TPU v7x, 32 devices: a whole 2x2x4 slice. The times are simulated.
32 devices in a mesh: lon: 4 (over x, core), lat: 8 (over z, y).
Axes of the slice: x: 2, y: 2, z: 4, core: 2. Of those that a mesh axis runs over, the one named last changes fastest.
Arguments:
- tracers: float32 [2, 20, 512, 1536], P(None, None, 'lat', 'lon'), may hold values from -6 to 6
- east_velocity: bfloat16 [20, 512, 1536], P(None, 'lat', 'lon'), may hold values from -3 to 3
- north_velocity: bfloat16 [20, 512, 1536], P(None, 'lat', 'lon'), may hold values from -3 to 3
- vertical_diffusivity: bfloat16 [20, 512, 1536], P(None, 'lat', 'lon'), may hold values from 0.049804688 to 5
- depth_levels: int32 [512, 1536], P('lat', 'lon'), may hold values from 0 to 20
- ocean_blocks: int32 [16, 8], P('lat', 'lon'), may hold values 0 or 1
- forcing: float32 [512, 1536], P('lat', 'lon'), may hold values from -6 to 6
- surface_coupling: float32 [512, 1536], P('lat', 'lon'), may hold values from 0.1 to 2
Outputs:
- new_tracers: float32 [2, 20, 512, 1536], P(None, None, 'lat', 'lon')
- surface_solution: float32 [512, 1536], P('lat', 'lon')
All inputs are finite; a program needn't handle non-finite values. No bound on the sum of `ocean_blocks` on one device may be relied on, other than what follows from the above.
Results may differ from a plain program's by a relative error of at most 0.0003.
Values sent between devices are 32-bit elements; how exact they have to be, the bound alone decides.
A program may use at most 192 MiB of HBM per device.

v0:
```python
import jax
import jax.numpy as jnp
from jax import lax
from jax.sharding import PartitionSpec as P

ITERS = 3


advection_rate = 0.25
biharmonic_rate = 0.01
corner_weight = 0.5


def extended_2(block, sides, width, periodic):
    for axis, dim in sides:
        count = lax.axis_size(axis)
        forward = [(i, i + 1) for i in range(count - 1)]
        if periodic:
            forward.append((count - 1, 0))
        backward = [(target, source) for source, target in forward]
        low = lax.ppermute(
            lax.slice_in_dim(block, block.shape[dim] - width, None, axis=dim), axis, forward
        )
        high = lax.ppermute(lax.slice_in_dim(block, 0, width, axis=dim), axis, backward)
        block = jnp.concatenate([low, block, high], axis=dim)
    return block


def from_partner(block, axis, stride):
    count = lax.axis_size(axis)
    route = []
    for low in range(count):
        high = low | 1 << stride
        if high != low and high < count:
            route += [(low, high), (high, low)]
    return lax.ppermute(block, axis, route)


def passed_along(value, axis, steps):
    count = lax.axis_size(axis)
    pairs = [(source, (source + steps) % count) for source in range(count)]
    return lax.ppermute(value, axis, pairs)


def shifted(shard, axis, by):
    count = lax.axis_size(axis)
    pairs = [(i, i + by) for i in range(count) if 0 <= i + by < count]
    return lax.ppermute(shard, axis, pairs)


def window(array, shift_row, shift_col):
    inner_height = array.shape[-2] - 2
    inner_width = array.shape[-1] - 2
    return array[..., shift_row : shift_row + inner_height, shift_col : shift_col + inner_width]


def masked_laplacian(values, wet_mask):
    centre = window(values, 1, 1)
    running = jnp.zeros_like(centre)
    for shift_row, shift_col in ((0, 1), (2, 1), (1, 0), (1, 2)):
        running = running + window(wet_mask, shift_row, shift_col) * (
            window(values, shift_row, shift_col) - centre
        )
    return window(wet_mask, 1, 1) * running


def face_flux(speed_one, speed_two, tracer_one, tracer_two, wet_one, wet_two):
    return 0.5 * (speed_one + speed_two) * 0.5 * (tracer_one + tracer_two) * wet_one * wet_two


def baroclinic(padded):
    tracer = padded[0:2]
    wet_mask = padded[2]
    inner_tracer = tracer[..., 1:-1, 1:-1]
    inner_mask = wet_mask[..., 1:-1, 1:-1]
    east_speed = padded[3][..., 1:-1, 1:-1]
    north_speed = padded[4][..., 1:-1, 1:-1]
    lap_one = masked_laplacian(tracer, wet_mask)
    lap_two = masked_laplacian(lap_one, inner_mask)
    centre = window(inner_tracer, 1, 1)
    wet_centre = window(inner_mask, 1, 1)
    east_flux = face_flux(
        window(east_speed, 1, 1),
        window(east_speed, 1, 2),
        centre,
        window(inner_tracer, 1, 2),
        wet_centre,
        window(inner_mask, 1, 2),
    )
    west_flux = face_flux(
        window(east_speed, 1, 0),
        window(east_speed, 1, 1),
        window(inner_tracer, 1, 0),
        centre,
        window(inner_mask, 1, 0),
        wet_centre,
    )
    north_flux = face_flux(
        window(north_speed, 1, 1),
        window(north_speed, 2, 1),
        centre,
        window(inner_tracer, 2, 1),
        wet_centre,
        window(inner_mask, 2, 1),
    )
    south_flux = face_flux(
        window(north_speed, 0, 1),
        window(north_speed, 1, 1),
        window(inner_tracer, 0, 1),
        centre,
        window(inner_mask, 0, 1),
        wet_centre,
    )
    divergence = east_flux - west_flux + north_flux - south_flux
    return wet_centre * (centre - advection_rate * divergence - biharmonic_rate * lap_two)


def vertical_mix(values, wet_mask, diffusivity):
    level_count = wet_mask.shape[0]
    zeros_plane = jnp.zeros_like(wet_mask[0])
    coupling = (
        [zeros_plane]
        + [diffusivity[k] * wet_mask[k] * wet_mask[k - 1] for k in range(1, level_count)]
        + [zeros_plane]
    )
    upper_ratio = []
    reduced = []
    for k in range(level_count):
        diagonal = 1.0 + coupling[k] + coupling[k + 1]
        if k == 0:
            divisor = diagonal
            source = values[:, 0]
        else:
            divisor = diagonal + coupling[k] * upper_ratio[k - 1]
            source = values[:, k] + coupling[k] * reduced[k - 1]
        upper_ratio.append(-coupling[k + 1] / divisor)
        reduced.append(source / divisor)
    result = [reduced[-1]]
    for k in range(level_count - 2, -1, -1):
        result.insert(0, reduced[k] - upper_ratio[k] * result[0])
    return jnp.stack(result, axis=1)


def nine_point(padded, wet_surface, centre_weight):
    centre = window(padded, 1, 1)
    edges = (
        window(padded, 0, 1) + window(padded, 2, 1) + window(padded, 1, 0) + window(padded, 1, 2)
    )
    corners = (
        window(padded, 0, 0) + window(padded, 0, 2) + window(padded, 2, 0) + window(padded, 2, 2)
    )
    return wet_surface * (centre_weight * centre - edges - corner_weight * corners)


def clinic_extend(stacked, fold_signs):
    row_count = stacked.shape[2]
    widened = extended_2(stacked, (("lon", 3),), 2, True)
    extended = extended_2(widened, (("lat", 2),), 2, False)
    top_rows = widened[:, :, row_count - 2 :, :]
    for bit in range(lax.axis_size("lon").bit_length() - 1):
        top_rows = from_partner(top_rows, "lon", bit)
    northern = jnp.flip(top_rows, axis=(2, 3)) * fold_signs
    at_top = lax.axis_index("lat") == lax.axis_size("lat") - 1
    ghost_rows = jnp.where(at_top, northern, extended[:, :, row_count + 2 :, :])
    return jnp.concatenate([extended[:, :, : row_count + 2, :], ghost_rows], axis=2)


def strip_pad(surface_field):
    lon_index = lax.axis_index("lon")
    lon_count = lax.axis_size("lon")
    first_row = surface_field[0:1, :]
    last_row = surface_field[-1:, :]
    following = passed_along(first_row, "lon", -1)
    following_far = shifted(following, "lat", -1)
    preceding = passed_along(last_row, "lon", 1)
    preceding_far = shifted(preceding, "lat", 1)
    above_row = jnp.where(lon_index == lon_count - 1, following_far, following)
    below_row = jnp.where(lon_index == 0, preceding_far, preceding)
    top_strip = jnp.logical_and(
        lon_index == lon_count - 1, lax.axis_index("lat") == lax.axis_size("lat") - 1
    )
    above_row = jnp.where(top_strip, jnp.flip(last_row, axis=1), above_row)
    extended = jnp.concatenate([below_row, surface_field, above_row], axis=0)
    return jnp.concatenate([extended[:, -1:], extended, extended[:, :1]], axis=1)


def paired_totals(residual, precond, operator_image):
    return lax.psum(
        (jnp.sum(residual * precond), jnp.sum(precond * operator_image)), ("lon", "lat")
    )


def solve(surface_source, wet_surface, centre_weight, padder):

    def apply_operator(surface_field):
        return nine_point(padder(surface_field), wet_surface, centre_weight)

    def precondition(residual):
        return wet_surface * residual / centre_weight

    solution = jnp.zeros_like(surface_source)
    residual = surface_source
    precond = precondition(residual)
    operator_image = apply_operator(precond)
    resid_dot, curvature = paired_totals(residual, precond, operator_image)
    step_size = resid_dot / curvature
    direction = precond
    direction_image = operator_image
    for iteration in range(ITERS):
        solution = solution + step_size * direction
        if iteration + 1 < ITERS:
            residual = residual - step_size * direction_image
            precond = precondition(residual)
            operator_image = apply_operator(precond)
            dot_next, curvature = paired_totals(residual, precond, operator_image)
            beta_ratio = dot_next / resid_dot
            step_size = dot_next / (curvature - beta_ratio * dot_next / step_size)
            direction = precond + beta_ratio * direction
            direction_image = operator_image + beta_ratio * direction_image
            resid_dot = dot_next
    return solution


def shards(
    tracers,
    east_velocity,
    north_velocity,
    vertical_diffusivity,
    depth_levels,
    ocean_blocks,
    forcing,
    surface_coupling,
):
    level_count = tracers.shape[1]
    row_count = tracers.shape[2]
    col_count = tracers.shape[3]
    ocean_cells = jnp.repeat(
        jnp.repeat(ocean_blocks, row_count // ocean_blocks.shape[0], axis=0),
        col_count // ocean_blocks.shape[1],
        axis=1,
    ).astype(jnp.float32)
    level_index = lax.broadcasted_iota(jnp.int32, (level_count, row_count, col_count), 0)
    wet_mask = jnp.where(
        level_index < depth_levels[None], ocean_cells[None], jnp.zeros_like(ocean_cells)[None]
    )
    east_float = east_velocity.astype(jnp.float32)
    north_float = north_velocity.astype(jnp.float32)
    stacked = jnp.concatenate(
        [tracers, wet_mask[None], east_float[None], north_float[None]], axis=0
    )
    fold_signs = jnp.array([1.0, 1.0, 1.0, -1.0, -1.0], jnp.float32).reshape(5, 1, 1, 1)
    padded = clinic_extend(stacked, fold_signs)
    provisional = baroclinic(padded)
    new_tracers = vertical_mix(provisional, wet_mask, vertical_diffusivity.astype(jnp.float32))
    wet_surface = wet_mask[0]
    surface_source = wet_surface * (forcing + jnp.mean(new_tracers[0] - new_tracers[1], axis=0))
    centre_weight = 6.0 + surface_coupling
    relaid = lax.all_to_all(
        jnp.stack([surface_source, wet_surface, centre_weight]),
        "lon",
        split_axis=1,
        concat_axis=2,
        tiled=True,
    )
    strip_solution = solve(relaid[0], relaid[1], relaid[2], strip_pad)
    solution = lax.all_to_all(strip_solution, "lon", split_axis=1, concat_axis=0, tiled=True)
    return (new_tracers, solution)


def solution(mesh):
    placed = (
        P(None, None, "lat", "lon"),
        P(None, "lat", "lon"),
        P(None, "lat", "lon"),
        P(None, "lat", "lon"),
        P("lat", "lon"),
        P("lat", "lon"),
        P("lat", "lon"),
        P("lat", "lon"),
    )
    return jax.shard_map(
        shards,
        mesh=mesh,
        in_specs=placed,
        out_specs=(P(None, None, "lat", "lon"), P("lat", "lon")),
        check_vma=False,
    )
```

profile of v0, /device:TPU:0, one launch (start us, length us, event | category | flops | bytes accessed | tf_op | source)
XLA Modules:
  0.0 472.5 jit_solution(13829028035563899560)
XLA Ops:
  4.5 3.4 pad_maximum_fusion.24
  7.9 3.7 copy.286
  11.6 2.4 collective-permute-start.1
  13.9 2.6 copy.285
  17.6 2.4 fusion.40
  35.2 2.6 copy.208
  37.9 3.4 copy.207
  41.3 3.1 pad_maximum_fusion.31
  47.8 4.2 collective-permute-start.2
  157.6 2.1 copy.211
  159.7 3.9 reverse
  165.3 13.5 %pad_maximum_fusion = f32[5,20,68,388]{3,2,1,0:T(8,128)S(1)} fusion(f32[5,20,2,388]{3,2,1,0:T(2,128)S(1)} %copy_select_fusion, f32[5,20,64,2]{3,2,1,0:T(8,128)S(1)} %copy.208, f32[1,20,64,384]{3,2,1,0:T(8,128)} %copy-done.6, f32[1,20,64,384]{3,2,1,0:T(8,128)} %copy-done.8, f32[1,20,64,384]{3,2,1,0:T(8,128)} %copy-done.10, f32[2,20,64,384]{3,2,1,0:T(8,128)} %param.9, ...), kind=kLoop, calls=%fused_computation | loop fusion | flops 18468800 | bytes 21107200 | tf_op jit(solution)/shard_map/concatenate | solution.py:165
  178.9 4.0 slice_bitcast_fusion.1
  182.9 2.9 copy-done
  185.8 8.3 %fusion.168 = (f32[20,66,386]{2,1,0:T(8,128)}, f32[20,66,386]{2,1,0:T(8,128)}, f32[20,66,386]{2,1,0:T(8,128)}, f32[20,66,386]{2,1,0:T(8,128)}, f32[20,66,386]{2,1,0:T(8,128)}) fusion(f32[20,68,388]{2,1,0:T(8,128)S(1)} %get-tuple-element.80), kind=kLoop, calls=%fused_computation.364 | loop fusion | bytes 20380800 | tf_op jit(solution)/shard_map/slice | solution.py:75
  194.1 6.4 %fusion.167 = (f32[20,64,384]{2,1,0:T(8,128)}, f32[20,64,384]{2,1,0:T(8,128)}, f32[20,64,384]{2,1,0:T(8,128)}, f32[20,64,384]{2,1,0:T(8,128)}, f32[20,64,384]{2,1,0:T(8,128)}) fusion(f32[20,68,388]{2,1,0:T(8,128)S(1)} %get-tuple-element.80), kind=kLoop, calls=%fused_computation.363 | loop fusion | bytes 19660800 | tf_op jit(solution)/shard_map/slice | solution.py:54
  200.5 7.8 %fusion.43 = (f32[20,64,384]{2,1,0:T(8,128)}, f32[20,64,384]{2,1,0:T(8,128)}) fusion(f32[20,68,388]{2,1,0:T(8,128)} %get-tuple-element.79), kind=kLoop, calls=%fused_computation.83 | loop fusion | flops 1966080 | bytes 9830400 | tf_op jit(solution)/shard_map/mul | solution.py:68
  208.3 3.6 fusion.45
  213.4 19.6 %fusion.2 = f32[2,20,66,386]{3,2,1,0:T(8,128)} fusion(f32[5,20,68,388]{3,2,1,0:T(8,128)} %copy-done, f32[5,20,2,388]{3,2,1,0:T(2,128)S(1)} %copy-done.15, f32[5,20,64,2]{3,2,1,0:T(8,128)S(1)} %copy-done.4, f32[5,20,64,2]{3,2,1,0:T(8,128)S(1)} %copy-done.5, f32[1,20,64,384]{3,2,1,0:T(8,128)S(1)} %copy-done.7, f32[1,20,64,384]{3,2,1,0:T(8,128)S(1)} %copy-done.9, ...), kind=kLoop, calls=%fused_computation.4 | loop fusion | flops 24456960 | bytes 37048640 | tf_op jit(solution)/shard_map/mul | solution.py:64
  233.0 32.9 %fusion.15 = f32[2,20,64,384]{3,2,1,0:T(8,128)} fusion(f32[2,20,66,386]{3,2,1,0:T(8,128)} %fusion.2, f32[2,20,64,384]{3,2,1,0:T(8,128)} %param.9, f32[5,20,2,388]{3,2,1,0:T(2,128)} %copy.214, f32[5,20,64,2]{3,2,1,0:T(8,128)S(1)} %copy-done.4, f32[5,20,64,2]{3,2,1,0:T(8,128)} %copy.207, f32[1,20,64,384]{3,2,1,0:T(8,128)} %copy-done.6, ...), kind=kLoop, calls=%fused_computation.31 | loop fusion | flops 55050240 | bytes 51841280 | tf_op jit(solution)/shard_map/mul | solution.py:115
  266.0 4.8 %subtract_dynamic-update-slice_fusion = (f32[2,20,64,384]{3,2,1,0:T(8,128)S(1)}, f32[2,1,64,384]{3,2,1,0:T(8,128)S(1)}, f32[2,1,64,384]{3,2,1,0:T(8,128)S(1)}, f...) fusion(f32[64,384]{1,0:T(8,128)} %copy.221, ...), kind=kLoop, calls=%fused_computation.181 | loop fusion | flops 4718591 | bytes 13369344
  277.6 9.8 %all_to_all.34 = f32[3,64,384]{2,0,1:T(4,128)S(1)} all-to-all(f32[3,64,384]{2,0,1:T(4,128)S(1)} %copy.281), channel_id=1, replica_groups=mesh['lon'=4,'lat'=8] {'lon'}, dimensions={1} | all-to-all | bytes 589824 | tf_op jit(solution)/shard_map/all_to_all | solution.py:258
  291.5 4.5 collective-permute-start.7
  298.5 4.2 collective-permute-done.9
  303.6 40.6 %all-reduce.2 = (f32[]{:T(128)}, f32[]{:T(128)}) all-reduce(f32[]{:T(128)} %get-tuple-element.116, f32[]{:T(128)} %get-tuple-element.17), channel_id=1, replica_groups=mesh['lon'=4,'lat'=8] {'lon','lat'}, use_global_device_ids=true, to_apply=%region_2.3 | all-reduce | flops 2 | bytes 16 | tf_op jit(solution)/shard_map/psum | solution.py:188
  348.6 4.4 collective-permute-start.11
  355.6 3.9 collective-permute-done.13
  360.5 40.2 %all-reduce.1 = (f32[]{:T(128)}, f32[]{:T(128)}) all-reduce(f32[]{:T(128)} %get-tuple-element.7, f32[]{:T(128)} %get-tuple-element.6), channel_id=1, replica_groups=mesh['lon'=4,'lat'=8] {'lon','lat'}, use_global_device_ids=true, to_apply=%region_6.7 | all-reduce | flops 2 | bytes 16 | tf_op jit(solution)/shard_map/psum | solution.py:188
  408.1 4.4 collective-permute-start.15
  414.9 4.2 collective-permute-done.17
  420.0 40.1 %all-reduce = (f32[]{:T(128)}, f32[]{:T(128)}) all-reduce(f32[]{:T(128)} %get-tuple-element.5, f32[]{:T(128)} %get-tuple-element.4), channel_id=1, replica_groups=mesh['lon'=4,'lat'=8] {'lon','lat'}, use_global_device_ids=true, to_apply=%region_10.11 | all-reduce | flops 2 | bytes 16 | tf_op jit(solution)/shard_map/psum | solution.py:188
  463.7 7.6 %all_to_all.35 = f32[16,4,384]{2,0,1:T(8,128)S(1)} all-to-all(f32[16,4,384]{2,0,1:T(8,128)S(1)} %bitcast.181), channel_id=1, replica_groups=mesh['lon'=4,'lat'=8] {'lon'}, dimensions={1} | all-to-all | bytes 196608 | tf_op jit(solution)/shard_map/all_to_all | solution.py:266
  (306 shorter events, 159.8 us)
Async XLA Ops:
  11.6 23.6 %collective-permute-start.1 = (f32[5,20,64,2]{2,1,3,0:T(8,128)}, f32[5,20,64,2]{2,1,3,0:T(8,128)}, u32[]{:S(2)}, u32[]{:S(2)}) collective-permute-start(f32[5,20,64,2]{2,1,3,0:T(8,128)} %copy.286), channel_id=1, source_target_pairs={{8,0},{16,8},{24,16},{0,24},{9,1},{17,9},{25,17},{1,25},{10,2},{18... | collective-permute-start | bytes 153608 | tf_op jit(solution)/shard_map/ppermute | solution.py:24
  16.5 21.3 %collective-permute-start = (f32[5,20,64,2]{2,1,3,0:T(8,128)}, f32[5,20,64,2]{2,1,3,0:T(8,128)}, u32[]{:S(2)}, u32[]{:S(2)}) collective-permute-start(f32[5,20,64,2]{2,1,3,0:T(8,128)} %copy.285), channel_id=1, source_target_pairs={{0,8},{8,16},{16,24},{24,0},{1,9},{9,17},{17,25},{25,1},{2,10},{10... | collective-permute-start | bytes 153608 | tf_op jit(solution)/shard_map/ppermute | solution.py:21
  37.8 127.5 %copy-start.3 = (f32[5,20,64,2]{3,2,1,0:T(8,128)}, f32[5,20,64,2]{3,2,1,0:T(8,128)S(1)}, u32[]{:S(2)}) copy-start(f32[5,20,64,2]{3,2,1,0:T(8,128)S(1)} %copy.208) | copy-start | bytes 153604
  41.2 5.5 %copy-start.26 = (f32[1,64,384]{1,2,0:T(8,128)S(1)}, f32[1,64,384]{1,2,0:T(8,128)}, u32[]{:S(2)}) copy-start(f32[1,64,384]{1,2,0:T(8,128)} %copy-done.25) | copy-start | bytes 294916
  44.4 11.5 %copy-start.39 = (f32[1,64,384]{1,2,0:T(8,128)S(1)}, f32[1,64,384]{1,2,0:T(8,128)}, u32[]{:S(2)}) copy-start(f32[1,64,384]{1,2,0:T(8,128)} %get-tuple-element.73) | copy-start | bytes 294916
  44.4 11.5 %copy-start.40 = (f32[1,64,384]{1,2,0:T(8,128)S(1)}, f32[1,64,384]{1,2,0:T(8,128)}, u32[]{:S(2)}) copy-start(f32[1,64,384]{1,2,0:T(8,128)} %get-tuple-element.74) | copy-start | bytes 294916
  45.3 9.0 %collective-permute-start.3 = (f32[5,20,2,388]{3,1,2,0:T(8,128)}, f32[5,20,2,388]{3,1,2,0:T(8,128)}, u32[]{:S(2)}, u32[]{:S(2)}) collective-permute-start(f32[5,20,2,388]{3,1,2,0:T(8,128)} %copy.209), channel_id=1, source_target_pairs={{0,8},{8,0},{16,24},{24,16},{1,9},{9,1},{17,25},{25,17},{2,10},{10... | collective-permute-start | bytes 931208 | tf_op jit(solution)/shard_map/ppermute | solution.py:36
  47.8 107.7 %collective-permute-start.2 = (f32[5,20,2,388]{3,1,2,0:T(8,128)}, f32[5,20,2,388]{3,1,2,0:T(8,128)}, u32[]{:S(2)}, u32[]{:S(2)}) collective-permute-start(f32[5,20,2,388]{3,1,2,0:T(8,128)} %copy.209), channel_id=1, source_target_pairs={{0,1},{1,2},{2,3},{3,4},{4,5},{5,6},{6,7},{8,9},{9,10},{10,11},{11... | collective-permute-start | bytes 931208 | tf_op jit(solution)/shard_map/ppermute | solution.py:21
  52.9 110.7 %collective-permute-start.5 = (f32[5,20,2,388]{3,1,2,0:T(8,128)}, f32[5,20,2,388]{3,1,2,0:T(8,128)}, u32[]{:S(2)}, u32[]{:S(2)}) collective-permute-start(f32[5,20,2,388]{3,1,2,0:T(8,128)} %copy.212), channel_id=1, source_target_pairs={{1,0},{2,1},{3,2},{4,3},{5,4},{6,5},{7,6},{9,8},{10,9},{11,10},{12... | collective-permute-start | bytes 931208 | tf_op jit(solution)/shard_map/ppermute | solution.py:24
  54.3 103.3 %collective-permute-start.4 = (f32[5,20,2,388]{3,1,2,0:T(8,128)}, f32[5,20,2,388]{3,1,2,0:T(8,128)}, u32[]{:S(2)}, u32[]{:S(2)}) collective-permute-start(f32[5,20,2,388]{3,1,2,0:T(8,128)} %collective-permute-done.3), channel_id=1, source_target_pairs={{0,16},{16,0},{8,24},{24,8},{1,17},{17,1},{9,25},{25,9},{2,18},{18... | collective-permute-start | bytes 931208 | tf_op jit(solution)/shard_map/ppermute | solution.py:36
  124.4 21.8 %copy-start.36 = (f32[1,64,384]{1,2,0:T(8,128)S(1)}, f32[1,64,384]{1,2,0:T(8,128)}, u32[]{:S(2)}) copy-start(f32[1,64,384]{1,2,0:T(8,128)} %copy-done.35) | copy-start | bytes 294916
  129.5 34.2 %copy-start.66 = (f32[5]{0:T(128)S(1)}, f32[5]{0:T(128)}, u32[]{:S(2)}) copy-start(f32[5]{0:T(128)} %constant.37.clone) | copy-start | bytes 64
  165.3 13.5 %copy-start.14 = (f32[5,20,2,388]{3,2,1,0:T(2,128)}, f32[5,20,2,388]{3,2,1,0:T(2,128)S(1)}, u32[]{:S(2)}) copy-start(f32[5,20,2,388]{3,2,1,0:T(2,128)S(1)} %copy_select_fusion) | copy-start | bytes 931204
  178.9 6.9 %copy-start = (f32[5,20,68,388]{3,2,1,0:T(8,128)}, f32[5,20,68,388]{3,2,1,0:T(8,128)S(1)}, u32[]{:S(2)}) copy-start(f32[5,20,68,388]{3,2,1,0:T(8,128)S(1)} %pad_maximum_fusion) | copy-start | bytes 31660804
  200.4 7.8 %copy-start.11 = (f32[20,68,388]{2,1,0:T(8,128)S(1)}, f32[20,68,388]{2,1,0:T(8,128)}, u32[]{:S(2)}) copy-start(f32[20,68,388]{2,1,0:T(8,128)} %get-tuple-element.78) | copy-start | bytes 6332164
  200.4 11.4 %copy-start.5 = (f32[5,20,64,2]{3,2,1,0:T(8,128)S(1)}, f32[5,20,64,2]{3,2,1,0:T(8,128)}, u32[]{:S(2)}) copy-start(f32[5,20,64,2]{3,2,1,0:T(8,128)} %copy.207) | copy-start | bytes 153604
  200.4 11.4 %copy-start.9 = (f32[1,20,64,384]{3,2,1,0:T(8,128)S(1)}, f32[1,20,64,384]{3,2,1,0:T(8,128)}, u32[]{:S(2)}) copy-start(f32[1,20,64,384]{3,2,1,0:T(8,128)} %copy-done.8) | copy-start | bytes 5898244
  200.4 11.4 %copy-start.15 = (f32[5,20,2,388]{3,2,1,0:T(2,128)S(1)}, f32[5,20,2,388]{3,2,1,0:T(2,128)}, u32[]{:S(2)}) copy-start(f32[5,20,2,388]{3,2,1,0:T(2,128)} %copy-done.14) | copy-start | bytes 931204
  233.0 32.9 %copy-start.50 = (f32[64,384]{1,0:T(8,128)S(1)}, f32[64,384]{1,0:T(8,128)}, u32[]{:S(2)}) copy-start(f32[64,384]{1,0:T(8,128)} %copy.277) | copy-start | bytes 294916
  233.0 32.9 %copy-start.51 = (f32[64,384]{1,0:T(8,128)S(1)}, f32[64,384]{1,0:T(8,128)}, u32[]{:S(2)}) copy-start(f32[64,384]{1,0:T(8,128)} %copy.276) | copy-start | bytes 294916
  288.4 3.1 collective-permute-start.6
  288.5 8.7 %collective-permute-start.8 = (f32[1,1536]{1,0:T(1,128)S(1)}, f32[1,1536]{1,0:T(1,128)S(1)}, u32[]{:S(2)}, u32[]{:S(2)}) collective-permute-start(f32[1,1536]{1,0:T(1,128)S(1)} %get-tuple-element.131), channel_id=1, source_target_pairs={{0,24},{8,0},{16,8},{24,16},{1,25},{9,1},{17,9},{25,17},{2,26},{10... | collective-permute-start | bytes 18440 | tf_op jit(solution)/shard_map/ppermute | solution.py:42
  291.5 6.9 %collective-permute-start.7 = (f32[1,1536]{1,0:T(1,128)S(1)}, f32[1,1536]{1,0:T(1,128)S(1)}, u32[]{:S(2)}, u32[]{:S(2)}) collective-permute-start(f32[1,1536]{1,0:T(1,128)S(1)} %collective-permute-done.6), channel_id=1, source_target_pairs={{0,1},{1,2},{2,3},{3,4},{4,5},{5,6},{6,7},{8,9},{9,10},{10,11},{11... | collective-permute-start | bytes 18440 | tf_op jit(solution)/shard_map/ppermute | solution.py:48
  297.1 5.5 %collective-permute-start.9 = (f32[1,1536]{1,0:T(1,128)S(1)}, f32[1,1536]{1,0:T(1,128)S(1)}, u32[]{:S(2)}, u32[]{:S(2)}) collective-permute-start(f32[1,1536]{1,0:T(1,128)S(1)} %collective-permute-done.8), channel_id=1, source_target_pairs={{1,0},{2,1},{3,2},{4,3},{5,4},{6,5},{7,6},{9,8},{10,9},{11,10},{12... | collective-permute-start | bytes 18440 | tf_op jit(solution)/shard_map/ppermute | solution.py:48
  345.5 3.1 collective-permute-start.10
  345.5 8.5 %collective-permute-start.12 = (f32[1,1536]{1,0:T(1,128)S(1)}, f32[1,1536]{1,0:T(1,128)S(1)}, u32[]{:S(2)}, u32[]{:S(2)}) collective-permute-start(f32[1,1536]{1,0:T(1,128)S(1)} %get-tuple-element.129), channel_id=1, source_target_pairs={{0,24},{8,0},{16,8},{24,16},{1,25},{9,1},{17,9},{25,17},{2,26},{10... | collective-permute-start | bytes 18440 | tf_op jit(solution)/shard_map/ppermute | solution.py:42
  348.6 7.0 %collective-permute-start.11 = (f32[1,1536]{1,0:T(1,128)S(1)}, f32[1,1536]{1,0:T(1,128)S(1)}, u32[]{:S(2)}, u32[]{:S(2)}) collective-permute-start(f32[1,1536]{1,0:T(1,128)S(1)} %collective-permute-done.10), channel_id=1, source_target_pairs={{0,1},{1,2},{2,3},{3,4},{4,5},{5,6},{6,7},{8,9},{9,10},{10,11},{11... | collective-permute-start | bytes 18440 | tf_op jit(solution)/shard_map/ppermute | solution.py:48
  354.0 5.5 %collective-permute-start.13 = (f32[1,1536]{1,0:T(1,128)S(1)}, f32[1,1536]{1,0:T(1,128)S(1)}, u32[]{:S(2)}, u32[]{:S(2)}) collective-permute-start(f32[1,1536]{1,0:T(1,128)S(1)} %collective-permute-done.12), channel_id=1, source_target_pairs={{1,0},{2,1},{3,2},{4,3},{5,4},{6,5},{7,6},{9,8},{10,9},{11,10},{12... | collective-permute-start | bytes 18440 | tf_op jit(solution)/shard_map/ppermute | solution.py:48
  405.0 3.1 collective-permute-start.14
  405.1 8.5 %collective-permute-start.16 = (f32[1,1536]{1,0:T(1,128)S(1)}, f32[1,1536]{1,0:T(1,128)S(1)}, u32[]{:S(2)}, u32[]{:S(2)}) collective-permute-start(f32[1,1536]{1,0:T(1,128)S(1)} %get-tuple-element.127), channel_id=1, source_target_pairs={{0,24},{8,0},{16,8},{24,16},{1,25},{9,1},{17,9},{25,17},{2,26},{10... | collective-permute-start | bytes 18440 | tf_op jit(solution)/shard_map/ppermute | solution.py:42
  408.1 6.8 %collective-permute-start.15 = (f32[1,1536]{1,0:T(1,128)S(1)}, f32[1,1536]{1,0:T(1,128)S(1)}, u32[]{:S(2)}, u32[]{:S(2)}) collective-permute-start(f32[1,1536]{1,0:T(1,128)S(1)} %collective-permute-done.14), channel_id=1, source_target_pairs={{0,1},{1,2},{2,3},{3,4},{4,5},{5,6},{6,7},{8,9},{9,10},{10,11},{11... | collective-permute-start | bytes 18440 | tf_op jit(solution)/shard_map/ppermute | solution.py:48
  413.6 5.5 %collective-permute-start.17 = (f32[1,1536]{1,0:T(1,128)S(1)}, f32[1,1536]{1,0:T(1,128)S(1)}, u32[]{:S(2)}, u32[]{:S(2)}) collective-permute-start(f32[1,1536]{1,0:T(1,128)S(1)} %collective-permute-done.16), channel_id=1, source_target_pairs={{1,0},{2,1},{3,2},{4,3},{5,4},{6,5},{7,6},{9,8},{10,9},{11,10},{12... | collective-permute-start | bytes 18440 | tf_op jit(solution)/shard_map/ppermute | solution.py:48
  (53 other events, 181.2 us)
where the time goes:
time: 482 us; the launch traced here: 473 us
  local copies, waits for them, and re-layouts  155 us (32%)
  blocking collectives  138 us (29%)
  other arithmetic  118 us (24%)
  starting transfers between devices  32.9 us (7%)
  waiting for transfers between devices  16.2 us (3%)
  between operations  11.2 us (2%)
    psum x3, blocking collectives, paired_totals(): lax.psum((jnp.sum(residual * precond), jnp.sum(precond * operator_image))...  121 us
    mul x1, other arithmetic, baroclinic(): wet_centre * (centre - advection_rate * divergence - biharmonic_rate * la...  32.9 us
    mul x19, local copies, waits for them, and re-layouts, vertical_mix(): source = values[:, k] + coupling[k] * reduced[k - 1]  31.9 us
    mul x19, local copies, waits for them, and re-layouts, vertical_mix(): result.insert(0, reduced[k] - upper_ratio[k] * result[0])  31.8 us
    div x20, local copies, waits for them, and re-layouts, vertical_mix(): reduced.append(source / divisor)  31.7 us
    unnamed x155, local copies, waits for them, and re-layouts  25 us
    mul x1, other arithmetic, masked_laplacian(): return window(wet_mask, 1, 1) * running  19.6 us
    ppermute x6, starting transfers between devices, shifted(): return lax.ppermute(shard, axis, pairs)  17.4 us
  transfers between devices with their start and end apart: 18, of which 6 were waited for; matrix products, arithmetic and copies ran while one was open for 29% of the time, Pallas kernels for 0%

commit v1 on v0

v1 whole, which is shorter than its diff:
```python
import functools

import jax
import jax.numpy as jnp
from jax import lax
from jax.experimental import pallas as pl
from jax.experimental.pallas import tpu as pltpu
from jax.sharding import PartitionSpec as P

F32 = jnp.float32
MESH = pl.DeviceIdType.MESH
VMEM = pl.BlockSpec(memory_space=pltpu.VMEM)
ANY = pl.BlockSpec(memory_space=pl.ANY)
PAD = 8
TILE = 128


def lane_index(shape):
    return lax.broadcasted_iota(jnp.int32, shape, len(shape) - 1)


def flip_tile(value):
    lane = lane_index(value.shape)
    for bit in range(7):
        step = 1 << bit
        value = jnp.where(
            lane & step != 0, pltpu.roll(value, step, 1), pltpu.roll(value, TILE - step, 1)
        )
    return value


def flip_row(value):
    tiles = value.shape[1] // TILE
    return jnp.concatenate(
        [flip_tile(value[:, t * TILE : (t + 1) * TILE]) for t in reversed(range(tiles))], axis=1
    )


def shift_lanes(value, by):
    width = value.shape[1]
    by = by % width
    return value if by == 0 else pltpu.roll(value, by, 1)


class Layout:
    def __init__(self, levels):
        self.levels = levels
        self.speed = 4 * levels
        self.depth = 5 * levels
        self.weight = 5 * levels + 3
        self.count = 5 * levels + 6
        self.rows = -(-self.count // 8) * 8


def copy_to(src, dst, send, recv, lon, lat):
    return pltpu.make_async_remote_copy(
        src_ref=src,
        dst_ref=dst,
        send_sem=send,
        recv_sem=recv,
        device_id={"lon": lon, "lat": lat},
        device_id_type=MESH,
    )


def greet(barrier, lon, lat):
    pl.semaphore_signal(barrier, inc=1, device_id={"lon": lon, "lat": lat}, device_id_type=MESH)


def ghost_kernel(
    lons, lats, levels,
    tr_ref, u_ref, v_ref, lev_ref, cw_ref,
    g_out, rs_out, rn_out,
    t_w, t_e, t_s, t_n, u_w, u_e, v_s, v_n,
    p_w, p_e, r_s, r_n, c_s, c_n, g_in, rs_in, rn_in,
    local_sem, send_sem, recv_sem,
):
    lay = Layout(levels)
    lon, lat = lax.axis_index("lon"), lax.axis_index("lat")
    rows, cols = lev_ref.shape
    east, west = lax.rem(lon + 1, lons), lax.rem(lon + lons - 1, lons)
    mirror = lons - 1 - lon
    top = lat == lats - 1
    bottom = lat == 0
    locals_ = [
        pltpu.make_async_copy(src, dst, local_sem.at[i])
        for i, (src, dst) in enumerate(
            (
                (tr_ref.at[:, :, 0:8, :], t_s),
                (tr_ref.at[:, :, rows - 8 : rows, :], t_n),
                (v_ref.at[:, 0:16, :], v_s),
                (v_ref.at[:, rows - 16 : rows, :], v_n),
                (tr_ref.at[:, :, :, 0:TILE], t_w),
                (tr_ref.at[:, :, :, cols - TILE : cols], t_e),
                (u_ref.at[:, :, 0:TILE], u_w),
                (u_ref.at[:, :, cols - TILE : cols], u_e),
            )
        )
    ]
    for copy in locals_:
        copy.start()
    barrier = pltpu.get_barrier_semaphore()
    greet(barrier, east, lat)
    greet(barrier, west, lat)

    @pl.when(top)
    def _():
        greet(barrier, mirror, lat)

    @pl.when(jnp.logical_not(top))
    def _():
        greet(barrier, lon, lat + 1)

    @pl.when(jnp.logical_not(bottom))
    def _():
        greet(barrier, lon, lat - 1)
        pl.semaphore_wait(barrier, 4)

    @pl.when(bottom)
    def _():
        pl.semaphore_wait(barrier, 3)
        rs_in[...] = jnp.zeros_like(rs_in)
        g_in[:, 0:PAD, :] = jnp.zeros_like(g_in[:, 0:PAD, :])

    for copy in locals_[0:4]:
        copy.wait()
    tail = 8 * (lay.depth // 8)
    r_s[tail:, :] = jnp.zeros_like(r_s[tail:, :])
    r_n[tail:, :] = jnp.zeros_like(r_n[tail:, :])
    for a in range(2):
        for k in range(levels):
            s = 2 * (a * levels + k)
            r_s[s : s + 2, :] = t_s[a, k, 0:2, :]
    for k in range(levels):
        r_s[lay.speed + k : lay.speed + k + 1, :] = v_s[k].astype(F32)[0:1, :]
    r_s[lay.depth : lay.depth + 3, :] = lev_ref[0:3, :]
    r_s[lay.weight : lay.weight + 3, :] = cw_ref[0:3, :]

    @pl.when(jnp.logical_not(top))
    def _():
        for a in range(2):
            for k in range(levels):
                s = 2 * (a * levels + k)
                r_n[s : s + 2, :] = t_n[a, k, 6:8, :]
        for k in range(levels):
            r_n[lay.speed + k : lay.speed + k + 1, :] = v_n[k].astype(F32)[15:16, :]
        r_n[lay.depth : lay.depth + 3, :] = lev_ref[rows - 3 : rows, :]
        r_n[lay.weight : lay.weight + 3, :] = cw_ref[rows - 3 : rows, :]

    @pl.when(top)
    def _():
        for a in range(2):
            for k in range(levels):
                s = 2 * (a * levels + k)
                r_n[s : s + 1, :] = t_n[a, k, 7:8, :]
                r_n[s + 1 : s + 2, :] = t_n[a, k, 6:7, :]
        for k in range(levels):
            r_n[lay.speed + k : lay.speed + k + 1, :] = -v_n[k].astype(F32)[15:16, :]
        for j in range(3):
            r_n[lay.depth + j : lay.depth + j + 1, :] = lev_ref[rows - 1 - j : rows - j, :]
            r_n[lay.weight + j : lay.weight + j + 1, :] = cw_ref[rows - 1 - j : rows - j, :]
        r_n[...] = flip_row(r_n[...])

    north_far = copy_to(r_n, rn_in, send_sem.at[0], recv_sem.at[0], mirror, lat)
    north_near = copy_to(r_n, rs_in, send_sem.at[0], recv_sem.at[1], lon, lat + 1)
    south = copy_to(r_s, rn_in, send_sem.at[1], recv_sem.at[0], lon, lat - 1)
    pl.when(top)(north_far.start)
    pl.when(jnp.logical_not(top))(north_near.start)
    pl.when(jnp.logical_not(bottom))(south.start)

    for copy in locals_[4:]:
        copy.wait()
    lane = lane_index((rows, TILE))
    back = TILE - 1 - lane
    first, last = jnp.zeros((rows, TILE), F32), jnp.zeros((rows, TILE), F32)
    for a in range(2):
        for k in range(levels):
            s = 2 * (a * levels + k)
            first = jnp.where(lane >> 1 == s // 2, shift_lanes(t_w[a, k], s), first)
            last = jnp.where(back >> 1 == s // 2, shift_lanes(t_e[a, k], -s), last)
    for k in range(levels):
        s = lay.speed + k
        first = jnp.where(lane == s, shift_lanes(u_w[k].astype(F32), s), first)
        last = jnp.where(back == s, shift_lanes(u_e[k].astype(F32), -s), last)
    for ref, s in ((lev_ref, lay.depth), (cw_ref, lay.weight)):
        inside = jnp.logical_and(lane >= s, lane < s + 3)
        first = jnp.where(inside, shift_lanes(ref[:, 0:TILE], s), first)
        inside = jnp.logical_and(back >= s, back < s + 3)
        last = jnp.where(inside, shift_lanes(ref[:, cols - TILE : cols], -s), last)
    p_w[...] = first
    p_e[...] = last
    own = slice(PAD, PAD + rows)
    to_west = copy_to(p_w, g_in.at[1, own, :], send_sem.at[2], recv_sem.at[2], west, lat)
    to_east = copy_to(p_e, g_in.at[0, own, :], send_sem.at[3], recv_sem.at[3], east, lat)
    to_west.start()
    to_east.start()
    to_west.wait_recv()
    to_east.wait_recv()
    c_s[...] = g_in[:, PAD : 2 * PAD, :]

    @pl.when(jnp.logical_not(top))
    def _():
        c_n[...] = g_in[:, rows : rows + PAD, :]

    @pl.when(top)
    def _():
        for side in range(2):
            turned = flip_tile(g_in[1 - side, rows : rows + PAD, :])
            for j in range(PAD):
                c_n[side, j : j + 1, :] = turned[PAD - 1 - j : PAD - j, :]

    high = g_in.at[:, PAD + rows : 2 * PAD + rows, :]
    low = g_in.at[:, 0:PAD, :]
    corner_far = copy_to(c_n, high, send_sem.at[4], recv_sem.at[4], mirror, lat)
    corner_near = copy_to(c_n, low, send_sem.at[4], recv_sem.at[5], lon, lat + 1)
    corner_south = copy_to(c_s, high, send_sem.at[5], recv_sem.at[4], lon, lat - 1)
    pl.when(top)(corner_far.start)
    pl.when(jnp.logical_not(top))(corner_near.start)
    pl.when(jnp.logical_not(bottom))(corner_south.start)

    north_far.wait_recv()
    rn_out[...] = rn_in[...]
    pl.when(jnp.logical_not(bottom))(north_near.wait_recv)
    rs_out[...] = rs_in[...]
    corner_far.wait_recv()
    pl.when(jnp.logical_not(bottom))(corner_near.wait_recv)
    g_out[...] = g_in[...]
    north_far.wait_send()
    corner_far.wait_send()
    to_west.wait_send()
    to_east.wait_send()
    pl.when(jnp.logical_not(bottom))(south.wait_send)
    pl.when(jnp.logical_not(bottom))(corner_south.wait_send)


def unpacked(g_ref, slot):
    lane = lane_index(g_ref.shape[1:])
    return jnp.where(
        lane < TILE // 2,
        pltpu.roll(g_ref[1], TILE - slot, 1),
        pltpu.roll(g_ref[0], slot, 1),
    )


def column_kernel(
    levels,
    tr_ref, u_ref, v_ref, kd_ref, lev_ref, forcing_ref, g_ref, rs_ref, rn_ref,
    out_ref, src_ref,
    tr, u, v, kd, vx, ux, lv, mk, q, lap, sm, ratio, red, coup,
    in_sem, out_sem,
):
    lay = Layout(levels)
    rows, cols = lev_ref.shape
    own = slice(PAD, PAD + rows)
    ghost = slice(cols, cols + TILE)

    def inputs(k):
        return (
            pltpu.make_async_copy(tr_ref.at[:, k], tr.at[:, k, own, 0:cols], in_sem.at[0, k]),
            pltpu.make_async_copy(u_ref.at[k], u.at[k], in_sem.at[1, k]),
            pltpu.make_async_copy(v_ref.at[k], v.at[k], in_sem.at[2, k]),
            pltpu.make_async_copy(kd_ref.at[k], kd.at[k], in_sem.at[3, k]),
        )

    def outputs(k):
        return pltpu.make_async_copy(red.at[:, k + 1], out_ref.at[:, k], out_sem.at[k])

    for k in range(levels):
        for copy in inputs(k):
            copy.start()
    for k in range(levels):
        for a in range(2):
            s = 2 * (a * levels + k)
            tr[a, k, PAD - 2 : PAD, 0:cols] = rs_ref[s : s + 2, :]
            tr[a, k, PAD + rows : PAD + rows + 2, 0:cols] = rn_ref[s : s + 2, :]
        s = lay.speed + k
        vx[k, PAD - 1 : PAD, :] = rs_ref[s : s + 1, :]
        vx[k, PAD + rows : PAD + rows + 1, :] = rn_ref[s : s + 1, :]
    lv[...] = jnp.zeros_like(lv)
    lv[own, 0:cols] = lev_ref[...]
    lv[PAD - 3 : PAD, 0:cols] = rs_ref[lay.depth : lay.depth + 3, :]
    lv[PAD + rows : PAD + rows + 3, 0:cols] = rn_ref[lay.depth : lay.depth + 3, :]
    lv[:, ghost] = unpacked(g_ref, lay.depth)
    coup[...] = jnp.zeros_like(coup)
    ratio[0] = jnp.zeros_like(ratio[0])
    red[:, 0] = jnp.zeros_like(red[:, 0])
    width = cols + TILE

    def right(value):
        return pltpu.roll(value, width - 1, 1)

    def left(value):
        return pltpu.roll(value, 1, 1)

    for copy in inputs(0):
        copy.wait()

    def down(k, carry):
        later = jnp.minimum(k + 1, levels - 1)

        @pl.when(k + 1 < levels)
        def _():
            for copy in inputs(later):
                copy.wait()

        level = k.astype(F32)
        ux[:, 0:cols] = u[k].astype(F32)
        ux[:, ghost] = unpacked(g_ref, lay.speed + k)[own]
        vx[k, own, :] = v[k].astype(F32)
        for a in range(2):
            tr[a, k, :, ghost] = unpacked(g_ref, 2 * (a * levels + k))
        for c in range(0, rows + 2 * PAD, 8):
            here = slice(c, c + 8)
            wet = jnp.where(lv[here] > level, 1.0, 0.0)
            mk[here] = wet
            for a in range(2):
                q[a, here] = wet * tr[a, k, here]
        for c in range(0, rows + 8, 8):
            base = c + PAD - 1
            wet = mk[base : base + 8]
            total = right(wet) + left(wet) + mk[base - 1 : base + 7] + mk[base + 1 : base + 9]
            sm[c : c + 8] = total
            for a in range(2):
                mid = q[a, base : base + 8]
                around = right(mid) + left(mid) + q[a, base - 1 : base + 7] + q[a, base + 1 : base + 9]
                lap[a, c : c + 8] = wet * (around - mid * total)
        for c in range(0, rows, 8):
            base = c + PAD
            here = slice(c, c + 8)
            wet_wide = mk[base : base + 8]
            wet = wet_wide[:, 0:cols]
            speed = ux[here]
            face = 0.25 * (speed + right(speed)) * (wet_wide * right(wet_wide))
            u_west = left(face)[:, 0:cols]
            u_east = face[:, 0:cols]
            v_mid = vx[k, base : base + 8]
            v_north = 0.25 * (v_mid + vx[k, base + 1 : base + 9]) * (wet * mk[base + 1 : base + 9, 0:cols])
            v_south = 0.25 * (v_mid + vx[k, base - 1 : base + 7]) * (wet * mk[base - 1 : base + 7, 0:cols])
            spread = u_east - u_west + v_north - v_south
            total = sm[c + 1 : c + 9, 0:cols]
            above = coup[here]
            below = kd[later, here].astype(F32) * jnp.where(lv[base : base + 8, 0:cols] > level + 1.0, 1.0, 0.0)
            inverse = 1.0 / (1.0 + above + below + above * ratio[k, here])
            ratio[k + 1, here] = -below * inverse
            coup[here] = below
            for a in range(2):
                wide = q[a, base : base + 8]
                mid = wide[:, 0:cols]
                divergence = (
                    mid * spread
                    + u_east * right(wide)[:, 0:cols]
                    - u_west * left(wide)[:, 0:cols]
                    + v_north * q[a, base + 1 : base + 9, 0:cols]
                    - v_south * q[a, base - 1 : base + 7, 0:cols]
                )
                lap_wide = lap[a, c + 1 : c + 9]
                around = (
                    right(lap_wide)[:, 0:cols]
                    + left(lap_wide)[:, 0:cols]
                    + lap[a, c + 2 : c + 10, 0:cols]
                    + lap[a, c : c + 8, 0:cols]
                )
                lap_two = wet * (around - lap_wide[:, 0:cols] * total)
                value = mid - 0.25 * divergence - 0.01 * lap_two
                red[a, k + 1, here] = (value + above * red[a, k, here]) * inverse
        return carry

    lax.fori_loop(0, levels, down, 0)
    outputs(levels - 1).start()
    coup[...] = red[0, levels] - red[1, levels]

    def up(i, carry):
        k = levels - 2 - i
        for c in range(0, rows, 8):
            here = slice(c, c + 8)
            factor = ratio[k + 1, here]
            one = red[0, k + 1, here] - factor * red[0, k + 2, here]
            two = red[1, k + 1, here] - factor * red[1, k + 2, here]
            red[0, k + 1, here] = one
            red[1, k + 1, here] = two
            coup[here] = coup[here] + (one - two)
        outputs(k).start()
        return carry

    lax.fori_loop(0, levels - 1, up, 0)
    src_ref[...] = jnp.where(
        lev_ref[...] > 0.0, forcing_ref[...] + coup[...] * (1.0 / levels), 0.0
    )
    for k in range(levels):
        outputs(k).wait()


def solve_kernel(
    lons, lats, levels,
    src_ref, lev_ref, cw_ref, g_ref, rs_ref, rn_ref,
    out_ref,
    lv, cw, bx, side_in, row_n, row_in, corner, corner_in, part, lon_in, joint, lat_in,
    send_sem, recv_sem, lon_send, lon_recv, lat_send, lat_recv,
):
    lay = Layout(levels)
    rows, cols = src_ref.shape
    lon, lat = lax.axis_index("lon"), lax.axis_index("lat")
    east, west = lax.rem(lon + 1, lons), lax.rem(lon + lons - 1, lons)
    mirror = lons - 1 - lon
    top = lat == lats - 1
    bottom = lat == 0
    own = slice(PAD, PAD + rows)
    north_rows = slice(PAD + rows, 2 * PAD + rows)
    ghost = slice(cols, cols + TILE)
    lon_peers = [lax.rem(lon + d, lons) for d in range(1, lons)]
    lat_peers = [lax.rem(lat + d, lats) for d in range(1, lats)]
    barrier = pltpu.get_barrier_semaphore()
    for peer in lon_peers:
        greet(barrier, peer, lat)
    for peer in lat_peers:
        greet(barrier, lon, peer)

    @pl.when(jnp.logical_not(top))
    def _():
        row_n[...] = src_ref[rows - 8 : rows, :]

    @pl.when(top)
    def _():
        turned = flip_row(src_ref[rows - 8 : rows, :])
        for j in range(8):
            row_n[j : j + 1, :] = turned[7 - j : 8 - j, :]

    @pl.when(bottom)
    def _():
        row_in[0] = jnp.zeros_like(row_in[0])
        corner_in[0] = jnp.zeros_like(corner_in[0])

    pl.semaphore_wait(barrier, lons - 1 + lats - 1)
    to_west = copy_to(src_ref.at[:, 0:TILE], side_in.at[1], send_sem.at[2], recv_sem.at[2], west, lat)
    to_east = copy_to(src_ref.at[:, cols - TILE : cols], side_in.at[0], send_sem.at[3], recv_sem.at[3], east, lat)
    to_west.start()
    to_east.start()
    north_far = copy_to(row_n, row_in.at[1], send_sem.at[0], recv_sem.at[0], mirror, lat)
    north_near = copy_to(row_n, row_in.at[0], send_sem.at[0], recv_sem.at[1], lon, lat + 1)
    south = copy_to(src_ref.at[0:8, :], row_in.at[1], send_sem.at[1], recv_sem.at[0], lon, lat - 1)
    pl.when(top)(north_far.start)
    pl.when(jnp.logical_not(top))(north_near.start)
    pl.when(jnp.logical_not(bottom))(south.start)

    for plane, own_ref, slot, empty in ((lv, lev_ref, lay.depth, 0.0), (cw, cw_ref, lay.weight, 1.0)):
        plane[...] = jnp.full(plane.shape, empty, F32)
        plane[own, 0:cols] = own_ref[...]
        plane[PAD - 3 : PAD, 0:cols] = rs_ref[slot : slot + 3, :]
        plane[PAD + rows : PAD + rows + 3, 0:cols] = rn_ref[slot : slot + 3, :]
        plane[:, ghost] = unpacked(g_ref, slot)
    wet = lv[...] > 0.0
    cw[...] = jnp.where(wet, cw[...], 1.0)
    lv[...] = jnp.where(wet, 1.0 / cw[...], 0.0)
    bx[own, 0:cols] = src_ref[...]

    to_west.wait_recv()
    to_east.wait_recv()
    lane = lane_index((rows, TILE))
    bx[own, ghost] = jnp.where(lane < TILE // 2, side_in[1], side_in[0])
    lane = lane_index((8, TILE))
    edge = bx[rows : rows + 8, ghost]
    corner[1] = bx[PAD : PAD + 8, ghost]

    @pl.when(jnp.logical_not(top))
    def _():
        corner[0] = edge

    @pl.when(top)
    def _():
        turned = flip_tile(edge)
        for j in range(8):
            corner[0, j : j + 1, :] = turned[7 - j : 8 - j, :]

    corner_far = copy_to(corner.at[0], corner_in.at[1], send_sem.at[4], recv_sem.at[4], mirror, lat)
    corner_near = copy_to(corner.at[0], corner_in.at[0], send_sem.at[4], recv_sem.at[5], lon, lat + 1)
    corner_south = copy_to(corner.at[1], corner_in.at[1], send_sem.at[5], recv_sem.at[4], lon, lat - 1)
    pl.when(top)(corner_far.start)
    pl.when(jnp.logical_not(top))(corner_near.start)
    pl.when(jnp.logical_not(bottom))(corner_south.start)
    north_far.wait_recv()
    bx[north_rows, 0:cols] = row_in[1]
    pl.when(jnp.logical_not(bottom))(north_near.wait_recv)
    bx[0:PAD, 0:cols] = row_in[0]
    corner_far.wait_recv()
    bx[north_rows, ghost] = corner_in[1]
    pl.when(jnp.logical_not(bottom))(corner_near.wait_recv)
    bx[0:PAD, ghost] = corner_in[0]

    height, width = bx.shape

    def operator(field):
        sides = pltpu.roll(field, 1, 1) + pltpu.roll(field, width - 1, 1)
        triple = field + 0.5 * sides
        ends = pltpu.roll(triple, 1, 0) + pltpu.roll(triple, height - 1, 0)
        return cw[...] * field - sides - ends

    zero = lv[...] * bx[...]
    image_zero = operator(zero)
    one = lv[...] * image_zero - zero
    image_one = operator(one)
    two = 2.0 * (lv[...] * image_one - one) - zero
    image_two = operator(two)

    def inner(value):
        return value[own, 0:cols]

    base = [inner(zero), inner(one), inner(two)]
    images = [inner(image_zero), inner(image_one), inner(image_two)]
    source = src_ref[...]
    pairs = [
        (base[0], images[0]), (base[1], images[0]), (base[2], images[0]),
        (base[1], images[1]), (base[2], images[1]), (base[2], images[2]),
        (base[0], source), (base[1], source), (base[2], source),
    ]
    part[8:16, :] = jnp.zeros((8, TILE), F32)
    for i, (x, y) in enumerate(pairs):
        line = jnp.sum(x * y, axis=0, keepdims=True)
        part[i : i + 1, :] = sum(line[:, t : t + TILE] for t in range(0, cols, TILE))
    over_lon = [
        copy_to(part, lon_in.at[d], lon_send.at[d], lon_recv.at[d], peer, lat)
        for d, peer in enumerate(lon_peers)
    ]
    for copy in over_lon:
        copy.start()
    for copy in over_lon:
        copy.wait_recv()
    joint[...] = part[...] + jnp.sum(lon_in[...], axis=0)
    over_lat = [
        copy_to(joint, lat_in.at[d], lat_send.at[d], lat_recv.at[d], lon, peer)
        for d, peer in enumerate(lat_peers)
    ]
    for copy in over_lat:
        copy.start()
    for copy in over_lat:
        copy.wait_recv()
    totals = jnp.sum(joint[...] + jnp.sum(lat_in[...], axis=0), axis=1, keepdims=True)
    g00, g01, g02, g11, g12, g22, d0, d1, d2 = (totals[i : i + 1, :] for i in range(9))
    small = 1e-9 * g00
    l10, l20 = g01 / g00, g02 / g00
    pivot_one = g11 - l10 * g01
    inverse_one = jnp.where(pivot_one > small, 1.0 / pivot_one, 0.0)
    cross = g12 - l20 * g01
    l21 = cross * inverse_one
    pivot_two = g22 - l20 * g02 - l21 * cross
    inverse_two = jnp.where(pivot_two > small, 1.0 / pivot_two, 0.0)
    y1 = d1 - l10 * d0
    y2 = d2 - l20 * d0 - l21 * y1
    c2 = y2 * inverse_two
    c1 = y1 * inverse_one - l21 * c2
    c0 = d0 / g00 - l10 * c1 - l20 * c2
    out_ref[...] = c0 * base[0] + c1 * base[1] + c2 * base[2]

    to_west.wait_send()
    to_east.wait_send()
    north_far.wait_send()
    corner_far.wait_send()
    pl.when(jnp.logical_not(bottom))(south.wait_send)
    pl.when(jnp.logical_not(bottom))(corner_south.wait_send)
    for copy in over_lon + over_lat:
        copy.wait_send()


def shards(
    lons, lats,
    tracers, east_velocity, north_velocity, vertical_diffusivity,
    depth_levels, ocean_blocks, forcing, surface_coupling,
):
    levels, rows, cols = tracers.shape[1:]
    lay = Layout(levels)
    ocean_cells = jnp.repeat(
        jnp.repeat(ocean_blocks, rows // ocean_blocks.shape[0], axis=0),
        cols // ocean_blocks.shape[1],
        axis=1,
    )
    depth = jnp.where(ocean_cells > 0, depth_levels, 0).astype(F32)
    weight = 6.0 + surface_coupling
    high, wide = rows + 2 * PAD, cols + TILE
    dma = pltpu.SemaphoreType.DMA
    strip = jax.ShapeDtypeStruct((lay.rows, cols), F32)
    bf16 = jnp.bfloat16
    ghosts, south, north = pl.pallas_call(
        functools.partial(ghost_kernel, lons, lats, levels),
        out_shape=(jax.ShapeDtypeStruct((2, high, TILE), F32), strip, strip),
        in_specs=[ANY, ANY, ANY, VMEM, VMEM],
        out_specs=(VMEM, VMEM, VMEM),
        scratch_shapes=[
            pltpu.VMEM((2, levels, rows, TILE), F32),
            pltpu.VMEM((2, levels, rows, TILE), F32),
            pltpu.VMEM((2, levels, 8, cols), F32),
            pltpu.VMEM((2, levels, 8, cols), F32),
            pltpu.VMEM((levels, rows, TILE), bf16),
            pltpu.VMEM((levels, rows, TILE), bf16),
            pltpu.VMEM((levels, 16, cols), bf16),
            pltpu.VMEM((levels, 16, cols), bf16),
            pltpu.VMEM((rows, TILE), F32),
            pltpu.VMEM((rows, TILE), F32),
            pltpu.VMEM((lay.rows, cols), F32),
            pltpu.VMEM((lay.rows, cols), F32),
            pltpu.VMEM((2, PAD, TILE), F32),
            pltpu.VMEM((2, PAD, TILE), F32),
            pltpu.VMEM((2, high, TILE), F32),
            pltpu.VMEM((lay.rows, cols), F32),
            pltpu.VMEM((lay.rows, cols), F32),
            dma((8,)), dma((6,)), dma((6,)),
        ],
        compiler_params=pltpu.CompilerParams(
            collective_id=0, has_side_effects=True, vmem_limit_bytes=32 << 20
        ),
        name="ghosts",
    )(tracers, east_velocity, north_velocity, depth, weight)
    new_tracers, source = pl.pallas_call(
        functools.partial(column_kernel, levels),
        out_shape=(
            jax.ShapeDtypeStruct(tracers.shape, F32),
            jax.ShapeDtypeStruct((rows, cols), F32),
        ),
        in_specs=[ANY] * 4 + [VMEM] * 5,
        out_specs=(ANY, VMEM),
        scratch_shapes=[
            pltpu.VMEM((2, levels, high, wide), F32),
            pltpu.VMEM((levels, rows, cols), bf16),
            pltpu.VMEM((levels, rows, cols), bf16),
            pltpu.VMEM((levels, rows, cols), bf16),
            pltpu.VMEM((levels, high, cols), F32),
            pltpu.VMEM((rows, wide), F32),
            pltpu.VMEM((high, wide), F32),
            pltpu.VMEM((high, wide), F32),
            pltpu.VMEM((2, high, wide), F32),
            pltpu.VMEM((2, high, wide), F32),
            pltpu.VMEM((high, wide), F32),
            pltpu.VMEM((levels + 1, rows, cols), F32),
            pltpu.VMEM((2, levels + 1, rows, cols), F32),
            pltpu.VMEM((rows, cols), F32),
            dma((4, levels)), dma((levels,)),
        ],
        compiler_params=pltpu.CompilerParams(vmem_limit_bytes=48 << 20),
        name="columns",
    )(tracers, east_velocity, north_velocity, vertical_diffusivity, depth, forcing, ghosts, south, north)
    surface = pl.pallas_call(
        functools.partial(solve_kernel, lons, lats, levels),
        out_shape=jax.ShapeDtypeStruct((rows, cols), F32),
        in_specs=[VMEM] * 6,
        out_specs=VMEM,
        scratch_shapes=[
            pltpu.VMEM((high, wide), F32),
            pltpu.VMEM((high, wide), F32),
            pltpu.VMEM((high, wide), F32),
            pltpu.VMEM((2, rows, TILE), F32),
            pltpu.VMEM((8, cols), F32),
            pltpu.VMEM((2, 8, cols), F32),
            pltpu.VMEM((2, 8, TILE), F32),
            pltpu.VMEM((2, 8, TILE), F32),
            pltpu.VMEM((16, TILE), F32),
            pltpu.VMEM((lons - 1, 16, TILE), F32),
            pltpu.VMEM((16, TILE), F32),
            pltpu.VMEM((lats - 1, 16, TILE), F32),
            dma((6,)), dma((6,)),
            dma((lons - 1,)), dma((lons - 1,)), dma((lats - 1,)), dma((lats - 1,)),
        ],
        compiler_params=pltpu.CompilerParams(
            collective_id=1, has_side_effects=True, vmem_limit_bytes=32 << 20
        ),
        name="surface",
    )(source, depth, weight, ghosts, south, north)
    return new_tracers, surface


def solution(mesh):
    flat = P("lat", "lon")
    deep = P(None, "lat", "lon")
    tracer = P(None, None, "lat", "lon")
    return jax.shard_map(
        functools.partial(shards, mesh.shape["lon"], mesh.shape["lat"]),
        mesh=mesh,
        in_specs=(tracer, deep, deep, deep, flat, flat, flat, flat),
        out_specs=(tracer, flat),
        check_vma=False,
    )
```

time: 482 us -> 71.7 us (0.15); the launches traced: 473 us -> 71.4 us
  local copies, waits for them, and re-layouts: 155 us -> 5.43 us
  blocking collectives: 138 us -> 0 us
  other arithmetic: 118 us -> 2.53 us
  Pallas kernels: 0 us -> 62.8 us
  starting transfers between devices: 32.9 us -> 0 us
  waiting for transfers between devices: 16.2 us -> 0 us
  between operations: 11.2 us -> 0.72 us
    psum x3 -> x0, blocking collectives: 121 us -> none  [paired_totals(): lax.psum((jnp.sum(residual * precond), jnp.sum(precond * operator_image))...]
    mul x15 -> x0, other arithmetic: 73.4 us -> none  [the longest x1 32.9 us: baroclinic(): wet_centre * (centre - advection_rate * divergence - biharmonic_rate * la...]
    mul x38 -> x0, local copies, waits for them, and re-layouts: 63.7 us -> none  [the longest x19 31.9 us: vertical_mix(): source = values[:, k] + coupling[k] * reduced[k - 1]]
    pallas_call x0 -> x3, Pallas kernels: none -> 62.8 us  [the longest x1 32.3 us: shards(): pl.pallas_call(functools.partial(column_kernel, levels), out_shape=(jax.S...]
    ppermute x18 -> x0, starting transfers between devices: 32.9 us -> none  [the longest x6 17.4 us: shifted(): return lax.ppermute(shard, axis, pairs)]
    div x20 -> x0, local copies, waits for them, and re-layouts: 31.7 us -> none  [vertical_mix(): reduced.append(source / divisor)]
    unnamed x155 -> x15, local copies, waits for them, and re-layouts: 25 us -> 5.17 us
    all_to_all x2 -> x0, blocking collectives: 17.5 us -> none  [the longest x1 9.84 us: shards(): lax.all_to_all(jnp.stack([surface_source, wet_surface, centre_weight]), '...]
  transfers between devices with their start and end apart: 18 -> 0, of which waited for: 6 -> 0; matrix products, arithmetic and copies ran while one was open for 29% -> 0% of each run, Pallas kernels for 0% -> 0%
where the time goes in v1:
time: 71.7 us; the launch traced here: 71.4 us
  Pallas kernels  62.8 us (88%)
  local copies, waits for them, and re-layouts  5.43 us (8%)
  other arithmetic  2.53 us (4%)
  between operations  0.72 us (1%)
    pallas_call x1, Pallas kernels, shards(): pl.pallas_call(functools.partial(column_kernel, levels), out_shape=(jax.S...  32.3 us
    pallas_call x1, Pallas kernels, shards(): pl.pallas_call(functools.partial(solve_kernel, lons, lats, levels), out_s...  18.5 us
    pallas_call x1, Pallas kernels, shards(): pl.pallas_call(functools.partial(ghost_kernel, lons, lats, levels), out_s...  12 us
    unnamed x15, local copies, waits for them, and re-layouts  5.17 us

profile of v1, /device:TPU:0, one launch (start us, length us, event | category | flops | bytes accessed | tf_op | source)
XLA Modules:
  0.0 71.4 jit_solution(16878431469593109690)
XLA Ops:
  0.6 0.0 copy-start.6
  0.6 0.7 %broadcast_compare_fusion = pred[2,2]{1,0:T(4,128)(4,1)S(1)} fusion(s32[2,2]{1,0:T(2,128)} %param.13), kind=kLoop, calls=%fused_computation.2 | loop fusion | flops 4 | bytes 20 | tf_op jit(solution)/shard_map/gt | solution.py:575
  1.4 0.1 broadcast_in_dim.9
  1.5 0.1 gt.19
  1.6 0.9 %select_convert_fusion.lev_ref = f32[64,384]{1,0:T(8,128)S(1)} fusion(pred[64,384]{1,0:T(8,128)(4,1)S(1)} %gt.19, s32[64,384]{1,0:T(8,128)} %param.12), kind=kLoop, calls=%fused_computation | loop fusion | flops 49152 | bytes 221184 | tf_op jit(solution)/shard_map/convert_element_type | solution.py:575
  2.5 0.9 %broadcast_add_fusion.cw_ref = f32[64,384]{1,0:T(8,128)S(1)} fusion(f32[64,384]{1,0:T(8,128)} %param.15), kind=kLoop, calls=%fused_computation.1 | loop fusion | flops 24576 | bytes 196608 | tf_op jit(solution)/shard_map/add | solution.py:576
  3.4 0.0 copy-start
  3.5 2.1 %copy-done = f32[2,20,64,384]{3,2,1,0:T(8,128)S(1)} copy-done((f32[2,20,64,384]{3,2,1,0:T(8,128)S(1)}, f32[2,20,64,384]{3,2,1,0:T(8,128)}, u32[]{:S(2)}) %copy-start) | copy-done | bytes 3932184
  5.6 0.0 copy-start.1
  5.6 1.2 %copy-done.1 = bf16[20,64,384]{2,1,0:T(8,128)(2,1)S(1)} copy-done((bf16[20,64,384]{2,1,0:T(8,128)(2,1)S(1)}, bf16[20,64,384]{2,1,0:T(8,128)(2,1)}, u32[]{:S(2)}) %copy-start.1) | copy-done | bytes 983064
  6.8 0.0 copy-start.3
  6.8 1.2 %copy-done.3 = bf16[20,64,384]{2,1,0:T(8,128)(2,1)S(1)} copy-done((bf16[20,64,384]{2,1,0:T(8,128)(2,1)S(1)}, bf16[20,64,384]{2,1,0:T(8,128)(2,1)}, u32[]{:S(2)}) %copy-start.3) | copy-done | bytes 983064
  8.0 0.0 copy-start.2
  8.0 0.0 copy-start.4
  8.0 0.0 copy-start.5
  8.0 12.0 %ghosts.1 = (f32[2,80,128]{2,1,0:T(8,128)S(1)}, f32[112,384]{1,0:T(8,128)S(1)}, f32[112,384]{1,0:T(8,128)S(1)}) custom-call(f32[2,20,64,384]{3,2,1,0:T(8,128)S(1)} %copy-done, bf16[20,64,384]{2,1,0:T(8,128)(2,1)S(1)} %copy-done.1, bf16[20,64,384]{2,1,0:T(8,128)(2,1)S(1)} %copy-done.3, f32[64,384]{1,0:T(8,128)S(1)} %select_convert_fusion.lev_ref, ...), custom_call_target="tpu_custom_call" | custom-call | tf_op jit(solution)/shard_map/ghosts/pallas_call | solution.py:581
  20.0 0.0 copy-done.6
  20.0 0.0 copy-done.2
  20.0 0.0 copy-done.4
  20.0 0.0 copy-done.5
  20.0 32.3 %columns.1 = (f32[2,20,64,384]{3,2,1,0:T(8,128)}, f32[64,384]{1,0:T(8,128)S(1)}) custom-call(f32[2,20,64,384]{3,2,1,0:T(8,128)} %tr_ref.3, bf16[20,64,384]{2,1,0:T(8,128)(2,1)S(1)} %copy-done.2, bf16[20,64,384]{2,1,0:T(8,128)(2,1)S(1)} %copy-done.4, bf16[20,64,384]{2,1,0:T(8,128)(2,1)S(1)} %copy-done.5, f32[64,384]{1,0:T(8,128)S(1)} %select_convert_fusion.lev_ref, ...), custom_call_target="tpu_custom_call" | custom-call | tf_op jit(solution)/shard_map/columns/pallas_call | solution.py:611
  52.3 18.5 %surface.1 = f32[64,384]{1,0:T(8,128)S(1)} custom-call(f32[64,384]{1,0:T(8,128)S(1)} %get-tuple-element.11.src_ref, f32[64,384]{1,0:T(8,128)S(1)} %select_convert_fusion.lev_ref, f32[64,384]{1,0:T(8,128)S(1)} %broadcast_add_fusion.cw_ref, f32[2,80,128]{2,1,0:T(8,128)S(1)} %get-tuple-element.7.g_ref, f32[112,384]{1,0:T(8,128)S(1)} %get-tuple-element.8.rs_ref, ...), custom_call_target="tpu_custom_call" | custom-call | tf_op jit(solution)/shard_map/surface/pallas_call | solution.py:639
  70.8 0.6 copy.17
  (1 shorter events, 0.0 us)
Async XLA Ops:
  0.6 19.3 %copy-start.6 = (f32[64,384]{1,0:T(8,128)S(1)}, f32[64,384]{1,0:T(8,128)}, u32[]{:S(2)}) copy-start(f32[64,384]{1,0:T(8,128)} %forcing_ref.1) | copy-start | bytes 294916
  3.4 2.1 %copy-start = (f32[2,20,64,384]{3,2,1,0:T(8,128)S(1)}, f32[2,20,64,384]{3,2,1,0:T(8,128)}, u32[]{:S(2)}) copy-start(f32[2,20,64,384]{3,2,1,0:T(8,128)} %tr_ref.3) | copy-start | bytes 11796484
  5.6 1.2 %copy-start.1 = (bf16[20,64,384]{2,1,0:T(8,128)(2,1)S(1)}, bf16[20,64,384]{2,1,0:T(8,128)(2,1)}, u32[]{:S(2)}) copy-start(bf16[20,64,384]{2,1,0:T(8,128)(2,1)} %u_ref.3) | copy-start | bytes 2949124
  6.8 1.2 %copy-start.3 = (bf16[20,64,384]{2,1,0:T(8,128)(2,1)S(1)}, bf16[20,64,384]{2,1,0:T(8,128)(2,1)}, u32[]{:S(2)}) copy-start(bf16[20,64,384]{2,1,0:T(8,128)(2,1)} %v_ref.3) | copy-start | bytes 2949124
  8.0 12.0 %copy-start.2 = (bf16[20,64,384]{2,1,0:T(8,128)(2,1)S(1)}, bf16[20,64,384]{2,1,0:T(8,128)(2,1)}, u32[]{:S(2)}) copy-start(bf16[20,64,384]{2,1,0:T(8,128)(2,1)} %u_ref.3) | copy-start | bytes 2949124
  8.0 12.0 %copy-start.4 = (bf16[20,64,384]{2,1,0:T(8,128)(2,1)S(1)}, bf16[20,64,384]{2,1,0:T(8,128)(2,1)}, u32[]{:S(2)}) copy-start(bf16[20,64,384]{2,1,0:T(8,128)(2,1)} %v_ref.3) | copy-start | bytes 2949124
  8.0 12.0 %copy-start.5 = (bf16[20,64,384]{2,1,0:T(8,128)(2,1)S(1)}, bf16[20,64,384]{2,1,0:T(8,128)(2,1)}, u32[]{:S(2)}) copy-start(bf16[20,64,384]{2,1,0:T(8,128)(2,1)} %kd_ref.1) | copy-start | bytes 2949124

commit v2 on v1

--- a/solution.py
+++ b/solution.py
@@ -10,7 +10,7 @@
 F32 = jnp.float32
 MESH = pl.DeviceIdType.MESH
 VMEM = pl.BlockSpec(memory_space=pltpu.VMEM)
-ANY = pl.BlockSpec(memory_space=pl.ANY)
+HBM = pl.BlockSpec(memory_space=pltpu.HBM)
 PAD = 8
 TILE = 128
 
@@ -67,17 +67,80 @@
     pl.semaphore_signal(barrier, inc=1, device_id={"lon": lon, "lat": lat}, device_id_type=MESH)
 
 
+class Corners:
+    def __init__(self, lons, lats, sources, turned, dst, send, recv):
+        lon, lat = lax.axis_index("lon"), lax.axis_index("lat")
+        east, west = lax.rem(lon + 1, lons), lax.rem(lon + lons - 1, lons)
+        self.top, self.bottom = lat == lats - 1, lat == 0
+        far_first, far_last = lax.rem(lons - lon, lons), lax.rem(2 * lons - 2 - lon, lons)
+        self.own_first = jnp.logical_and(self.top, far_first == lon)
+        self.own_last = jnp.logical_and(self.top, far_last == lon)
+        self.turned, self.dst = turned, dst
+        high_first, high_last, low_first, low_last = sources
+        turned_first, turned_last = turned
+        self.up_last = copy_to(high_last, dst.at[0, 0], send.at[0], recv.at[0], east, lat + 1)
+        self.up_first = copy_to(high_first, dst.at[0, 1], send.at[1], recv.at[1], west, lat + 1)
+        self.far_first = copy_to(turned_first, dst.at[1, 0], send.at[1], recv.at[2], far_first, lat)
+        self.far_last = copy_to(turned_last, dst.at[1, 1], send.at[0], recv.at[3], far_last, lat)
+        self.down_last = copy_to(low_last, dst.at[1, 0], send.at[2], recv.at[2], east, lat - 1)
+        self.down_first = copy_to(low_first, dst.at[1, 1], send.at[3], recv.at[3], west, lat - 1)
+
+    def start(self):
+        @pl.when(jnp.logical_not(self.top))
+        def _():
+            self.up_last.start()
+            self.up_first.start()
+
+        @pl.when(jnp.logical_not(self.bottom))
+        def _():
+            self.down_last.start()
+            self.down_first.start()
+
+        pl.when(jnp.logical_and(self.top, jnp.logical_not(self.own_first)))(self.far_first.start)
+        pl.when(jnp.logical_and(self.top, jnp.logical_not(self.own_last)))(self.far_last.start)
+
+        @pl.when(self.own_first)
+        def _():
+            self.dst[1, 0] = self.turned[0][...]
+
+        @pl.when(self.own_last)
+        def _():
+            self.dst[1, 1] = self.turned[1][...]
+
+        @pl.when(self.bottom)
+        def _():
+            self.dst[0] = jnp.zeros_like(self.dst[0])
+
+    def wait_recv(self):
+        @pl.when(jnp.logical_not(self.bottom))
+        def _():
+            self.up_last.wait_recv()
+            self.up_first.wait_recv()
+
+        pl.when(jnp.logical_not(self.own_first))(self.far_first.wait_recv)
+        pl.when(jnp.logical_not(self.own_last))(self.far_last.wait_recv)
+
+    def wait_send(self):
+        pl.when(jnp.logical_not(self.own_last))(self.up_last.wait_send)
+        pl.when(jnp.logical_not(self.own_first))(self.up_first.wait_send)
+
+        @pl.when(jnp.logical_not(self.bottom))
+        def _():
+            self.down_last.wait_send()
+            self.down_first.wait_send()
+
+
 def ghost_kernel(
     lons, lats, levels,
-    tr_ref, u_ref, v_ref, lev_ref, cw_ref,
-    g_out, rs_out, rn_out,
+    tr_ref, u_ref, v_ref, depth_ref, ocean_ref, coupling_ref,
+    g_out, rs_out, rn_out, lev_ref, cw_ref,
     t_w, t_e, t_s, t_n, u_w, u_e, v_s, v_n,
-    p_w, p_e, r_s, r_n, c_s, c_n, g_in, rs_in, rn_in,
-    local_sem, send_sem, recv_sem,
+    p_w, p_e, r_s, r_n, turned, corner_in, g_in, rs_in, rn_in,
+    local_sem, send_sem, recv_sem, corner_send, corner_recv,
 ):
     lay = Layout(levels)
     lon, lat = lax.axis_index("lon"), lax.axis_index("lat")
-    rows, cols = lev_ref.shape
+    rows, cols = depth_ref.shape
     east, west = lax.rem(lon + 1, lons), lax.rem(lon + lons - 1, lons)
     mirror = lons - 1 - lon
     top = lat == lats - 1
@@ -107,21 +170,33 @@
     def _():
         greet(barrier, mirror, lat)
 
+        greet(barrier, lax.rem(lons - lon, lons), lat)
+        greet(barrier, lax.rem(2 * lons - 2 - lon, lons), lat)
+
     @pl.when(jnp.logical_not(top))
     def _():
-        greet(barrier, lon, lat + 1)
+        for peer in (lon, east, west):
+            greet(barrier, peer, lat + 1)
 
     @pl.when(jnp.logical_not(bottom))
     def _():
-        greet(barrier, lon, lat - 1)
-        pl.semaphore_wait(barrier, 4)
+        for peer in (lon, east, west):
+            greet(barrier, peer, lat - 1)
 
     @pl.when(bottom)
     def _():
-        pl.semaphore_wait(barrier, 3)
         rs_in[...] = jnp.zeros_like(rs_in)
-        g_in[:, 0:PAD, :] = jnp.zeros_like(g_in[:, 0:PAD, :])
-
+
+    row = lax.broadcasted_iota(jnp.int32, (rows, cols), 0)
+    col = lane_index((rows, cols))
+    tall, broad = rows // ocean_ref.shape[0], cols // ocean_ref.shape[1]
+    cells = jnp.zeros((rows, cols), jnp.int32)
+    for i in range(ocean_ref.shape[0]):
+        for j in range(ocean_ref.shape[1]):
+            inside = (row >= i * tall) & (row < (i + 1) * tall) & (col >= j * broad) & (col < (j + 1) * broad)
+            cells = jnp.where(inside, ocean_ref[i, j], cells)
+    lev_ref[...] = jnp.where(cells > 0, depth_ref[...], 0).astype(F32)
+    cw_ref[...] = 6.0 + coupling_ref[...]
     for copy in locals_[0:4]:
         copy.wait()
     tail = 8 * (lay.depth // 8)
@@ -160,6 +235,18 @@
             r_n[lay.depth + j : lay.depth + j + 1, :] = lev_ref[rows - 1 - j : rows - j, :]
             r_n[lay.weight + j : lay.weight + j + 1, :] = cw_ref[rows - 1 - j : rows - j, :]
         r_n[...] = flip_row(r_n[...])
+
+    @pl.when(bottom)
+    def _():
+        pl.semaphore_wait(barrier, 5)
+
+    @pl.when(top)
+    def _():
+        pl.semaphore_wait(barrier, 8)
+
+    @pl.when(jnp.logical_not(jnp.logical_or(top, bottom)))
+    def _():
+        pl.semaphore_wait(barrier, 8)
 
     north_far = copy_to(r_n, rn_in, send_sem.at[0], recv_sem.at[0], mirror, lat)
     north_near = copy_to(r_n, rs_in, send_sem.at[0], recv_sem.at[1], lon, lat + 1)
@@ -190,47 +277,40 @@
     p_w[...] = first
     p_e[...] = last
     own = slice(PAD, PAD + rows)
-    to_west = copy_to(p_w, g_in.at[1, own, :], send_sem.at[2], recv_sem.at[2], west, lat)
-    to_east = copy_to(p_e, g_in.at[0, own, :], send_sem.at[3], recv_sem.at[3], east, lat)
+    to_west = copy_to(p_w, g_in.at[1], send_sem.at[2], recv_sem.at[2], west, lat)
+    to_east = copy_to(p_e, g_in.at[0], send_sem.at[3], recv_sem.at[3], east, lat)
     to_west.start()
     to_east.start()
-    to_west.wait_recv()
-    to_east.wait_recv()
-    c_s[...] = g_in[:, PAD : 2 * PAD, :]
-
-    @pl.when(jnp.logical_not(top))
-    def _():
-        c_n[...] = g_in[:, rows : rows + PAD, :]
 
     @pl.when(top)
     def _():
-        for side in range(2):
-            turned = flip_tile(g_in[1 - side, rows : rows + PAD, :])
+        for side, value in enumerate((first, last)):
+            back_tile = flip_tile(value[rows - PAD : rows, :])
             for j in range(PAD):
-                c_n[side, j : j + 1, :] = turned[PAD - 1 - j : PAD - j, :]
-
-    high = g_in.at[:, PAD + rows : 2 * PAD + rows, :]
-    low = g_in.at[:, 0:PAD, :]
-    corner_far = copy_to(c_n, high, send_sem.at[4], recv_sem.at[4], mirror, lat)
-    corner_near = copy_to(c_n, low, send_sem.at[4], recv_sem.at[5], lon, lat + 1)
-    corner_south = copy_to(c_s, high, send_sem.at[5], recv_sem.at[4], lon, lat - 1)
-    pl.when(top)(corner_far.start)
-    pl.when(jnp.logical_not(top))(corner_near.start)
-    pl.when(jnp.logical_not(bottom))(corner_south.start)
-
+                turned[side, j : j + 1, :] = back_tile[PAD - 1 - j : PAD - j, :]
+
+    corners = Corners(
+        lons, lats,
+        (p_w.at[rows - PAD : rows, :], p_e.at[rows - PAD : rows, :], p_w.at[0:PAD, :], p_e.at[0:PAD, :]),
+        (turned.at[0], turned.at[1]),
+        corner_in, corner_send, corner_recv,
+    )
+    corners.start()
     north_far.wait_recv()
     rn_out[...] = rn_in[...]
     pl.when(jnp.logical_not(bottom))(north_near.wait_recv)
     rs_out[...] = rs_in[...]
-    corner_far.wait_recv()
-    pl.when(jnp.logical_not(bottom))(corner_near.wait_recv)
-    g_out[...] = g_in[...]
+    to_west.wait_recv()
+    to_east.wait_recv()
+    g_out[:, own, :] = g_in[...]
+    corners.wait_recv()
+    g_out[:, 0:PAD, :] = corner_in[0]
+    g_out[:, PAD + rows : 2 * PAD + rows, :] = corner_in[1]
     north_far.wait_send()
-    corner_far.wait_send()
     to_west.wait_send()
     to_east.wait_send()
     pl.when(jnp.logical_not(bottom))(south.wait_send)
-    pl.when(jnp.logical_not(bottom))(corner_south.wait_send)
+    corners.wait_send()
 
 
 def unpacked(g_ref, slot):
@@ -251,6 +331,7 @@
 ):
     lay = Layout(levels)
     rows, cols = lev_ref.shape
+    tiles = cols // TILE
     own = slice(PAD, PAD + rows)
     ghost = slice(cols, cols + TILE)
 
@@ -274,23 +355,31 @@
             tr[a, k, PAD - 2 : PAD, 0:cols] = rs_ref[s : s + 2, :]
             tr[a, k, PAD + rows : PAD + rows + 2, 0:cols] = rn_ref[s : s + 2, :]
         s = lay.speed + k
-        vx[k, PAD - 1 : PAD, :] = rs_ref[s : s + 1, :]
-        vx[k, PAD + rows : PAD + rows + 1, :] = rn_ref[s : s + 1, :]
-    lv[...] = jnp.zeros_like(lv)
-    lv[own, 0:cols] = lev_ref[...]
-    lv[PAD - 3 : PAD, 0:cols] = rs_ref[lay.depth : lay.depth + 3, :]
-    lv[PAD + rows : PAD + rows + 3, 0:cols] = rn_ref[lay.depth : lay.depth + 3, :]
-    lv[:, ghost] = unpacked(g_ref, lay.depth)
+        for t in range(tiles):
+            part = slice(t * TILE, (t + 1) * TILE)
+            vx[k, t, PAD - 1 : PAD, :] = rs_ref[s : s + 1, part]
+            vx[k, t, PAD + rows : PAD + rows + 1, :] = rn_ref[s : s + 1, part]
+    for t in range(tiles):
+        part = slice(t * TILE, (t + 1) * TILE)
+        lv[t, 0:PAD] = jnp.zeros((PAD, TILE), F32)
+        lv[t, PAD + rows :] = jnp.zeros((PAD, TILE), F32)
+        lv[t, own] = lev_ref[:, part]
+        lv[t, PAD - 3 : PAD] = rs_ref[lay.depth : lay.depth + 3, part]
+        lv[t, PAD + rows : PAD + rows + 3] = rn_ref[lay.depth : lay.depth + 3, part]
+    lv[tiles] = unpacked(g_ref, lay.depth)
     coup[...] = jnp.zeros_like(coup)
     ratio[0] = jnp.zeros_like(ratio[0])
     red[:, 0] = jnp.zeros_like(red[:, 0])
-    width = cols + TILE
-
-    def right(value):
-        return pltpu.roll(value, width - 1, 1)
-
-    def left(value):
-        return pltpu.roll(value, 1, 1)
+    lane = lane_index((8, TILE))
+    lane_last, lane_first = lane == TILE - 1, lane == 0
+
+    def right(parts):
+        turned = [pltpu.roll(x, TILE - 1, 1) for x in parts]
+        return [jnp.where(lane_last, turned[(t + 1) % (tiles + 1)], turned[t]) for t in range(tiles + 1)]
+
+    def left(parts):
+        turned = [pltpu.roll(x, 1, 1) for x in parts]
+        return [jnp.where(lane_first, turned[(t + tiles) % (tiles + 1)], turned[t]) for t in range(tiles + 1)]
 
     for copy in inputs(0):
         copy.wait()
@@ -304,65 +393,74 @@
                 copy.wait()
 
         level = k.astype(F32)
-        ux[:, 0:cols] = u[k].astype(F32)
-        ux[:, ghost] = unpacked(g_ref, lay.speed + k)[own]
-        vx[k, own, :] = v[k].astype(F32)
+        for t in range(tiles):
+            ux[t] = u[k, :, t * TILE : (t + 1) * TILE].astype(F32)
+            vx[k, t, own] = v[k, :, t * TILE : (t + 1) * TILE].astype(F32)
+        ux[tiles] = unpacked(g_ref, lay.speed + k)[own]
         for a in range(2):
             tr[a, k, :, ghost] = unpacked(g_ref, 2 * (a * levels + k))
         for c in range(0, rows + 2 * PAD, 8):
             here = slice(c, c + 8)
-            wet = jnp.where(lv[here] > level, 1.0, 0.0)
-            mk[here] = wet
-            for a in range(2):
-                q[a, here] = wet * tr[a, k, here]
+            for t in range(tiles + 1):
+                wet = jnp.where(lv[t, here] > level, 1.0, 0.0)
+                mk[t, here] = wet
+                for a in range(2):
+                    q[a, t, here] = wet * tr[a, k, here, t * TILE : (t + 1) * TILE]
+        every = range(tiles + 1)
         for c in range(0, rows + 8, 8):
             base = c + PAD - 1
-            wet = mk[base : base + 8]
-            total = right(wet) + left(wet) + mk[base - 1 : base + 7] + mk[base + 1 : base + 9]
-            sm[c : c + 8] = total
+            mid, low, high = slice(base, base + 8), slice(base - 1, base + 7), slice(base + 1, base + 9)
+            wet = [mk[t, mid] for t in every]
+            e, w = right(wet), left(wet)
+            total = [e[t] + w[t] + mk[t, low] + mk[t, high] for t in every]
+            for t in every:
+                sm[t, c : c + 8] = total[t]
             for a in range(2):
-                mid = q[a, base : base + 8]
-                around = right(mid) + left(mid) + q[a, base - 1 : base + 7] + q[a, base + 1 : base + 9]
-                lap[a, c : c + 8] = wet * (around - mid * total)
+                centre = [q[a, t, mid] for t in every]
+                e, w = right(centre), left(centre)
+                for t in every:
+                    around = e[t] + w[t] + q[a, t, low] + q[a, t, high]
+                    lap[a, t, c : c + 8] = wet[t] * (around - centre[t] * total[t])
         for c in range(0, rows, 8):
             base = c + PAD
+            mid, low, high = slice(base, base + 8), slice(base - 1, base + 7), slice(base + 1, base + 9)
             here = slice(c, c + 8)
-            wet_wide = mk[base : base + 8]
-            wet = wet_wide[:, 0:cols]
-            speed = ux[here]
-            face = 0.25 * (speed + right(speed)) * (wet_wide * right(wet_wide))
-            u_west = left(face)[:, 0:cols]
-            u_east = face[:, 0:cols]
-            v_mid = vx[k, base : base + 8]
-            v_north = 0.25 * (v_mid + vx[k, base + 1 : base + 9]) * (wet * mk[base + 1 : base + 9, 0:cols])
-            v_south = 0.25 * (v_mid + vx[k, base - 1 : base + 7]) * (wet * mk[base - 1 : base + 7, 0:cols])
-            spread = u_east - u_west + v_north - v_south
-            total = sm[c + 1 : c + 9, 0:cols]
-            above = coup[here]
-            below = kd[later, here].astype(F32) * jnp.where(lv[base : base + 8, 0:cols] > level + 1.0, 1.0, 0.0)
-            inverse = 1.0 / (1.0 + above + below + above * ratio[k, here])
-            ratio[k + 1, here] = -below * inverse
-            coup[here] = below
-            for a in range(2):
-                wide = q[a, base : base + 8]
-                mid = wide[:, 0:cols]
-                divergence = (
-                    mid * spread
-                    + u_east * right(wide)[:, 0:cols]
-                    - u_west * left(wide)[:, 0:cols]
-                    + v_north * q[a, base + 1 : base + 9, 0:cols]
-                    - v_south * q[a, base - 1 : base + 7, 0:cols]
-                )
-                lap_wide = lap[a, c + 1 : c + 9]
-                around = (
-                    right(lap_wide)[:, 0:cols]
-                    + left(lap_wide)[:, 0:cols]
-                    + lap[a, c + 2 : c + 10, 0:cols]
-                    + lap[a, c : c + 8, 0:cols]
-                )
-                lap_two = wet * (around - lap_wide[:, 0:cols] * total)
-                value = mid - 0.25 * divergence - 0.01 * lap_two
-                red[a, k + 1, here] = (value + above * red[a, k, here]) * inverse
+            if c % 16 == 0:
+                mixing = kd[later, c : c + 16].astype(F32)
+            wet = [mk[t, mid] for t in every]
+            speed = [ux[t, here] for t in every]
+            wet_e, speed_e = right(wet), right(speed)
+            face = [0.25 * (speed[t] + speed_e[t]) * (wet[t] * wet_e[t]) for t in every]
+            face_w = left(face)
+            wide = [[q[a, t, mid] for t in every] for a in range(2)]
+            wide_e, wide_w = [right(x) for x in wide], [left(x) for x in wide]
+            bent = [[lap[a, t, c + 1 : c + 9] for t in every] for a in range(2)]
+            bent_e, bent_w = [right(x) for x in bent], [left(x) for x in bent]
+            for t in range(tiles):
+                part = slice(t * TILE, (t + 1) * TILE)
+                v_mid = vx[k, t, mid]
+                v_north = 0.25 * (v_mid + vx[k, t, high]) * (wet[t] * mk[t, high])
+                v_south = 0.25 * (v_mid + vx[k, t, low]) * (wet[t] * mk[t, low])
+                spread = face[t] - face_w[t] + v_north - v_south
+                total = sm[t, c + 1 : c + 9]
+                above = coup[here, part]
+                below = jnp.where(lv[t, mid] > level + 1.0, mixing[c % 16 : c % 16 + 8, part], 0.0)
+                inverse = 1.0 / (1.0 + above + below + above * ratio[k, here, part])
+                ratio[k + 1, here, part] = -below * inverse
+                coup[here, part] = below
+                for a in range(2):
+                    centre = wide[a][t]
+                    divergence = (
+                        centre * spread
+                        + face[t] * wide_e[a][t]
+                        - face_w[t] * wide_w[a][t]
+                        + v_north * q[a, t, high]
+                        - v_south * q[a, t, low]
+                    )
+                    around = bent_e[a][t] + bent_w[a][t] + lap[a, t, c + 2 : c + 10] + lap[a, t, c : c + 8]
+                    lap_two = wet[t] * (around - bent[a][t] * total)
+                    value = centre - 0.25 * divergence - 0.01 * lap_two
+                    red[a, k + 1, here, part] = (value + above * red[a, k, here, part]) * inverse
         return carry
 
     lax.fori_loop(0, levels, down, 0)
@@ -394,8 +492,8 @@
     lons, lats, levels,
     src_ref, lev_ref, cw_ref, g_ref, rs_ref, rn_ref,
     out_ref,
-    lv, cw, bx, side_in, row_n, row_in, corner, corner_in, part, lon_in, joint, lat_in,
-    send_sem, recv_sem, lon_send, lon_recv, lat_send, lat_recv,
+    lv, cw, bx, side_in, row_n, row_in, corner_in, part, lon_in, joint, lat_in,
+    send_sem, recv_sem, corner_send, corner_recv, lon_send, lon_recv, lat_send, lat_recv,
 ):
     lay = Layout(levels)
     rows, cols = src_ref.shape
@@ -417,6 +515,16 @@
 
     @pl.when(jnp.logical_not(top))
     def _():
+        greet(barrier, east, lat + 1)
+        greet(barrier, west, lat + 1)
+
+    @pl.when(jnp.logical_not(bottom))
+    def _():
+        greet(barrier, east, lat - 1)
+        greet(barrier, west, lat - 1)
+
+    @pl.when(jnp.logical_not(top))
+    def _():
         row_n[...] = src_ref[rows - 8 : rows, :]
 
     @pl.when(top)
@@ -428,9 +536,17 @@
     @pl.when(bottom)
     def _():
         row_in[0] = jnp.zeros_like(row_in[0])
-        corner_in[0] = jnp.zeros_like(corner_in[0])
-
-    pl.semaphore_wait(barrier, lons - 1 + lats - 1)
+
+    peers = lons - 1 + lats - 1
+
+    @pl.when(jnp.logical_or(top, bottom))
+    def _():
+        pl.semaphore_wait(barrier, peers + 2)
+
+    @pl.when(jnp.logical_not(jnp.logical_or(top, bottom)))
+    def _():
+        pl.semaphore_wait(barrier, peers + 4)
+
     to_west = copy_to(src_ref.at[:, 0:TILE], side_in.at[1], send_sem.at[2], recv_sem.at[2], west, lat)
     to_east = copy_to(src_ref.at[:, cols - TILE : cols], side_in.at[0], send_sem.at[3], recv_sem.at[3], east, lat)
     to_west.start()
@@ -442,6 +558,16 @@
     pl.when(jnp.logical_not(top))(north_near.start)
     pl.when(jnp.logical_not(bottom))(south.start)
 
+    corners = Corners(
+        lons, lats,
+        (
+            src_ref.at[rows - 8 : rows, 0:TILE], src_ref.at[rows - 8 : rows, cols - TILE : cols],
+            src_ref.at[0:8, 0:TILE], src_ref.at[0:8, cols - TILE : cols],
+        ),
+        (row_n.at[:, cols - TILE : cols], row_n.at[:, 0:TILE]),
+        corner_in, corner_send, corner_recv,
+    )
+    corners.start()
     for plane, own_ref, slot, empty in ((lv, lev_ref, lay.depth, 0.0), (cw, cw_ref, lay.weight, 1.0)):
         plane[...] = jnp.full(plane.shape, empty, F32)
         plane[own, 0:cols] = own_ref[...]
@@ -457,34 +583,14 @@
     to_east.wait_recv()
     lane = lane_index((rows, TILE))
     bx[own, ghost] = jnp.where(lane < TILE // 2, side_in[1], side_in[0])
-    lane = lane_index((8, TILE))
-    edge = bx[rows : rows + 8, ghost]
-    corner[1] = bx[PAD : PAD + 8, ghost]
-
-    @pl.when(jnp.logical_not(top))
-    def _():
-        corner[0] = edge
-
-    @pl.when(top)
-    def _():
-        turned = flip_tile(edge)
-        for j in range(8):
-            corner[0, j : j + 1, :] = turned[7 - j : 8 - j, :]
-
-    corner_far = copy_to(corner.at[0], corner_in.at[1], send_sem.at[4], recv_sem.at[4], mirror, lat)
-    corner_near = copy_to(corner.at[0], corner_in.at[0], send_sem.at[4], recv_sem.at[5], lon, lat + 1)
-    corner_south = copy_to(corner.at[1], corner_in.at[1], send_sem.at[5], recv_sem.at[4], lon, lat - 1)
-    pl.when(top)(corner_far.start)
-    pl.when(jnp.logical_not(top))(corner_near.start)
-    pl.when(jnp.logical_not(bottom))(corner_south.start)
     north_far.wait_recv()
     bx[north_rows, 0:cols] = row_in[1]
     pl.when(jnp.logical_not(bottom))(north_near.wait_recv)
     bx[0:PAD, 0:cols] = row_in[0]
-    corner_far.wait_recv()
-    bx[north_rows, ghost] = corner_in[1]
-    pl.when(jnp.logical_not(bottom))(corner_near.wait_recv)
-    bx[0:PAD, ghost] = corner_in[0]
+    corners.wait_recv()
+    lane = lane_index((8, TILE))
+    bx[north_rows, ghost] = jnp.where(lane < TILE // 2, corner_in[1, 1], corner_in[1, 0])
+    bx[0:PAD, ghost] = jnp.where(lane < TILE // 2, corner_in[0, 1], corner_in[0, 0])
 
     height, width = bx.shape
 
@@ -553,9 +659,8 @@
     to_west.wait_send()
     to_east.wait_send()
     north_far.wait_send()
-    corner_far.wait_send()
     pl.when(jnp.logical_not(bottom))(south.wait_send)
-    pl.when(jnp.logical_not(bottom))(corner_south.wait_send)
+    corners.wait_send()
     for copy in over_lon + over_lat:
         copy.wait_send()
 
@@ -567,22 +672,16 @@
 ):
     levels, rows, cols = tracers.shape[1:]
     lay = Layout(levels)
-    ocean_cells = jnp.repeat(
-        jnp.repeat(ocean_blocks, rows // ocean_blocks.shape[0], axis=0),
-        cols // ocean_blocks.shape[1],
-        axis=1,
-    )
-    depth = jnp.where(ocean_cells > 0, depth_levels, 0).astype(F32)
-    weight = 6.0 + surface_coupling
-    high, wide = rows + 2 * PAD, cols + TILE
+    high, wide, tiles = rows + 2 * PAD, cols + TILE, cols // TILE
     dma = pltpu.SemaphoreType.DMA
     strip = jax.ShapeDtypeStruct((lay.rows, cols), F32)
     bf16 = jnp.bfloat16
-    ghosts, south, north = pl.pallas_call(
+    plane = jax.ShapeDtypeStruct((rows, cols), F32)
+    ghosts, south, north, depth, weight = pl.pallas_call(
         functools.partial(ghost_kernel, lons, lats, levels),
-        out_shape=(jax.ShapeDtypeStruct((2, high, TILE), F32), strip, strip),
-        in_specs=[ANY, ANY, ANY, VMEM, VMEM],
-        out_specs=(VMEM, VMEM, VMEM),
+        out_shape=(jax.ShapeDtypeStruct((2, high, TILE), F32), strip, strip, plane, plane),
+        in_specs=[HBM, HBM, HBM, VMEM, pl.BlockSpec(memory_space=pltpu.SMEM), VMEM],
+        out_specs=(VMEM,) * 5,
         scratch_shapes=[
             pltpu.VMEM((2, levels, rows, TILE), F32),
             pltpu.VMEM((2, levels, rows, TILE), F32),
@@ -597,37 +696,37 @@
             pltpu.VMEM((lay.rows, cols), F32),
             pltpu.VMEM((lay.rows, cols), F32),
             pltpu.VMEM((2, PAD, TILE), F32),
-            pltpu.VMEM((2, PAD, TILE), F32),
-            pltpu.VMEM((2, high, TILE), F32),
+            pltpu.VMEM((2, 2, PAD, TILE), F32),
+            pltpu.VMEM((2, rows, TILE), F32),
             pltpu.VMEM((lay.rows, cols), F32),
             pltpu.VMEM((lay.rows, cols), F32),
-            dma((8,)), dma((6,)), dma((6,)),
+            dma((8,)), dma((4,)), dma((4,)), dma((4,)), dma((4,)),
         ],
         compiler_params=pltpu.CompilerParams(
             collective_id=0, has_side_effects=True, vmem_limit_bytes=32 << 20
         ),
         name="ghosts",
-    )(tracers, east_velocity, north_velocity, depth, weight)
+    )(tracers, east_velocity, north_velocity, depth_levels, ocean_blocks, surface_coupling)
     new_tracers, source = pl.pallas_call(
         functools.partial(column_kernel, levels),
         out_shape=(
             jax.ShapeDtypeStruct(tracers.shape, F32),
             jax.ShapeDtypeStruct((rows, cols), F32),
         ),
-        in_specs=[ANY] * 4 + [VMEM] * 5,
-        out_specs=(ANY, VMEM),
+        in_specs=[HBM] * 4 + [VMEM] * 5,
+        out_specs=(HBM, VMEM),
         scratch_shapes=[
             pltpu.VMEM((2, levels, high, wide), F32),
             pltpu.VMEM((levels, rows, cols), bf16),
             pltpu.VMEM((levels, rows, cols), bf16),
             pltpu.VMEM((levels, rows, cols), bf16),
-            pltpu.VMEM((levels, high, cols), F32),
-            pltpu.VMEM((rows, wide), F32),
-            pltpu.VMEM((high, wide), F32),
-            pltpu.VMEM((high, wide), F32),
-            pltpu.VMEM((2, high, wide), F32),
-            pltpu.VMEM((2, high, wide), F32),
-            pltpu.VMEM((high, wide), F32),
+            pltpu.VMEM((levels, tiles, high, TILE), F32),
+            pltpu.VMEM((tiles + 1, rows, TILE), F32),
+            pltpu.VMEM((tiles + 1, high, TILE), F32),
+            pltpu.VMEM((tiles + 1, high, TILE), F32),
+            pltpu.VMEM((2, tiles + 1, high, TILE), F32),
+            pltpu.VMEM((2, tiles + 1, high, TILE), F32),
+            pltpu.VMEM((tiles + 1, high, TILE), F32),
             pltpu.VMEM((levels + 1, rows, cols), F32),
             pltpu.VMEM((2, levels + 1, rows, cols), F32),
             pltpu.VMEM((rows, cols), F32),
@@ -648,13 +747,12 @@
             pltpu.VMEM((2, rows, TILE), F32),
             pltpu.VMEM((8, cols), F32),
             pltpu.VMEM((2, 8, cols), F32),
-            pltpu.VMEM((2, 8, TILE), F32),
-            pltpu.VMEM((2, 8, TILE), F32),
+            pltpu.VMEM((2, 2, 8, TILE), F32),
             pltpu.VMEM((16, TILE), F32),
             pltpu.VMEM((lons - 1, 16, TILE), F32),
             pltpu.VMEM((16, TILE), F32),
             pltpu.VMEM((lats - 1, 16, TILE), F32),
-            dma((6,)), dma((6,)),
+            dma((4,)), dma((4,)), dma((4,)), dma((4,)),
             dma((lons - 1,)), dma((lons - 1,)), dma((lats - 1,)), dma((lats - 1,)),
         ],
         compiler_params=pltpu.CompilerParams(

time: 71.7 us -> 69.7 us (0.972)
  other arithmetic: 2.53 us -> 0 us
  local copies, waits for them, and re-layouts: 5.43 us -> 7.63 us
  Pallas kernels: 62.8 us -> 61 us
    pallas_call x1, Pallas kernels: 18.5 us -> 15.5 us  [shards(): pl.pallas_call(functools.partial(solve_kernel, lons, lats, levels), out_s...]
    unnamed x15 -> x21, local copies, waits for them, and re-layouts: 5.17 us -> 7.63 us
    pallas_call x1, Pallas kernels: 12 us -> 13.4 us  [shards(): pl.pallas_call(functools.partial(ghost_kernel, lons, lats, levels), out_s...]
    convert_element_type x1 -> x0, other arithmetic: 0.91 us -> none  [shards(): depth = jnp.where(ocean_cells > 0, depth_levels, 0).astype(F32)]
    add x1 -> x0, other arithmetic: 0.9 us -> none  [shards(): weight = 6.0 + surface_coupling]
    gt x1 -> x0, other arithmetic: 0.72 us -> none  [shards(): depth = jnp.where(ocean_cells > 0, depth_levels, 0).astype(F32)]
where the time goes in v2:
time: 69.7 us; the launch traced here: 69.4 us
  Pallas kernels  61 us (88%)
  local copies, waits for them, and re-layouts  7.63 us (11%)
  between operations  0.71 us (1%)
    pallas_call x1, Pallas kernels, shards(): pl.pallas_call(functools.partial(column_kernel, levels), out_shape=(jax.S...  32.1 us
    pallas_call x1, Pallas kernels, shards(): pl.pallas_call(functools.partial(solve_kernel, lons, lats, levels), out_s...  15.5 us
    pallas_call x1, Pallas kernels, shards(): pl.pallas_call(functools.partial(ghost_kernel, lons, lats, levels), out_s...  13.4 us
    unnamed x21, local copies, waits for them, and re-layouts  7.63 us

profile of v2, /device:TPU:0, one launch (start us, length us, event | category | flops | bytes accessed | tf_op | source)
XLA Modules:
  0.0 69.4 jit_solution(12329551780589595214)
XLA Ops:
  0.6 0.0 copy-start
  0.6 2.1 %copy-done = f32[2,20,64,384]{3,2,1,0:T(8,128)S(1)} copy-done((f32[2,20,64,384]{3,2,1,0:T(8,128)S(1)}, f32[2,20,64,384]{3,2,1,0:T(8,128)}, u32[]{:S(2)}) %copy-start) | copy-done | bytes 3932184
  2.7 0.0 copy-start.1
  2.8 1.2 %copy-done.1 = bf16[20,64,384]{2,1,0:T(8,128)(2,1)S(1)} copy-done((bf16[20,64,384]{2,1,0:T(8,128)(2,1)S(1)}, bf16[20,64,384]{2,1,0:T(8,128)(2,1)}, u32[]{:S(2)}) %copy-start.1) | copy-done | bytes 983064
  4.0 0.0 copy-start.3
  4.0 1.2 %copy-done.3 = bf16[20,64,384]{2,1,0:T(8,128)(2,1)S(1)} copy-done((bf16[20,64,384]{2,1,0:T(8,128)(2,1)S(1)}, bf16[20,64,384]{2,1,0:T(8,128)(2,1)}, u32[]{:S(2)}) %copy-start.3) | copy-done | bytes 983064
  5.2 0.0 copy-start.7
  5.2 0.9 %copy-done.7 = s32[64,384]{1,0:T(8,128)S(1)} copy-done((s32[64,384]{1,0:T(8,128)S(1)}, s32[64,384]{1,0:T(8,128)}, u32[]{:S(2)}) %copy-start.7) | copy-done | bytes 98328
  6.0 0.0 copy-start.8
  6.0 0.9 %copy-done.8 = f32[64,384]{1,0:T(8,128)S(1)} copy-done((f32[64,384]{1,0:T(8,128)S(1)}, f32[64,384]{1,0:T(8,128)}, u32[]{:S(2)}) %copy-start.8) | copy-done | bytes 98328
  6.9 0.0 copy-start.9
  6.9 0.7 copy-done.9
  7.6 0.0 copy-start.2
  7.6 0.0 copy-start.4
  7.6 0.0 copy-start.5
  7.6 0.0 copy-start.6
  7.6 13.4 %ghosts.1 = (f32[2,80,128]{2,1,0:T(8,128)S(1)}, f32[112,384]{1,0:T(8,128)S(1)}, f32[112,384]{1,0:T(8,128)S(1)}, f32[64,384]{1,0:T(8,128)S(1)}, f32[64,384]{1,0:T(8,128)S(1)}) custom-call(f32[2,20,64,384]{3,2,1,0:T(8,128)S(1)} %copy-done, bf16[20,64,384]{2,1,0:T(8,128)(2,1)S(1)} %copy-done.1, bf16[20,64,384]{2,1,0:T(8,128)(2,1)S(1)} %copy-done.3, ...), custom_call_target="tpu_custom_call" | custom-call | tf_op jit(solution)/shard_map/ghosts/pallas_call | solution.py:680
  21.1 0.0 copy-done.2
  21.1 0.0 copy-done.4
  21.1 0.0 copy-done.5
  21.1 0.0 copy-done.6
  21.1 32.1 %columns.1 = (f32[2,20,64,384]{3,2,1,0:T(8,128)}, f32[64,384]{1,0:T(8,128)S(1)}) custom-call(f32[2,20,64,384]{3,2,1,0:T(8,128)} %tr_ref.3, bf16[20,64,384]{2,1,0:T(8,128)(2,1)S(1)} %copy-done.2, bf16[20,64,384]{2,1,0:T(8,128)(2,1)S(1)} %copy-done.4, bf16[20,64,384]{2,1,0:T(8,128)(2,1)S(1)} %copy-done.5, f32[64,384]{1,0:T(8,128)S(1)} %get-tuple-element.9.lev_ref, ...), custom_call_target="tpu_custom_call" | custom-call | tf_op jit(solution)/shard_map/columns/pallas_call | solution.py:710
  53.2 15.5 %surface.1 = f32[64,384]{1,0:T(8,128)S(1)} custom-call(f32[64,384]{1,0:T(8,128)S(1)} %get-tuple-element.14.src_ref, f32[64,384]{1,0:T(8,128)S(1)} %get-tuple-element.9.lev_ref, f32[64,384]{1,0:T(8,128)S(1)} %get-tuple-element.15.cw_ref, f32[2,80,128]{2,1,0:T(8,128)S(1)} %get-tuple-element.10.g_ref, f32[112,384]{1,0:T(8,128)S(1)} %get-tuple-element.11.rs_ref, ...), custom_call_target="tpu_custom_call" | custom-call | tf_op jit(solution)/shard_map/surface/pallas_call | solution.py:738
  68.7 0.6 copy.11
Async XLA Ops:
  0.6 2.1 %copy-start = (f32[2,20,64,384]{3,2,1,0:T(8,128)S(1)}, f32[2,20,64,384]{3,2,1,0:T(8,128)}, u32[]{:S(2)}) copy-start(f32[2,20,64,384]{3,2,1,0:T(8,128)} %tr_ref.3) | copy-start | bytes 11796484
  2.7 1.2 %copy-start.1 = (bf16[20,64,384]{2,1,0:T(8,128)(2,1)S(1)}, bf16[20,64,384]{2,1,0:T(8,128)(2,1)}, u32[]{:S(2)}) copy-start(bf16[20,64,384]{2,1,0:T(8,128)(2,1)} %u_ref.3) | copy-start | bytes 2949124
  4.0 1.2 %copy-start.3 = (bf16[20,64,384]{2,1,0:T(8,128)(2,1)S(1)}, bf16[20,64,384]{2,1,0:T(8,128)(2,1)}, u32[]{:S(2)}) copy-start(bf16[20,64,384]{2,1,0:T(8,128)(2,1)} %v_ref.3) | copy-start | bytes 2949124
  5.2 0.9 %copy-start.7 = (s32[64,384]{1,0:T(8,128)S(1)}, s32[64,384]{1,0:T(8,128)}, u32[]{:S(2)}) copy-start(s32[64,384]{1,0:T(8,128)} %depth_ref.1) | copy-start | bytes 294916
  6.0 0.9 %copy-start.8 = (f32[64,384]{1,0:T(8,128)S(1)}, f32[64,384]{1,0:T(8,128)}, u32[]{:S(2)}) copy-start(f32[64,384]{1,0:T(8,128)} %coupling_ref.1) | copy-start | bytes 294916
  6.9 0.7 copy-start.9
  7.6 13.5 %copy-start.2 = (bf16[20,64,384]{2,1,0:T(8,128)(2,1)S(1)}, bf16[20,64,384]{2,1,0:T(8,128)(2,1)}, u32[]{:S(2)}) copy-start(bf16[20,64,384]{2,1,0:T(8,128)(2,1)} %u_ref.3) | copy-start | bytes 2949124
  7.6 13.5 %copy-start.4 = (bf16[20,64,384]{2,1,0:T(8,128)(2,1)S(1)}, bf16[20,64,384]{2,1,0:T(8,128)(2,1)}, u32[]{:S(2)}) copy-start(bf16[20,64,384]{2,1,0:T(8,128)(2,1)} %v_ref.3) | copy-start | bytes 2949124
  7.6 13.5 %copy-start.5 = (bf16[20,64,384]{2,1,0:T(8,128)(2,1)S(1)}, bf16[20,64,384]{2,1,0:T(8,128)(2,1)}, u32[]{:S(2)}) copy-start(bf16[20,64,384]{2,1,0:T(8,128)(2,1)} %kd_ref.1) | copy-start | bytes 2949124
  7.6 13.5 %copy-start.6 = (f32[64,384]{1,0:T(8,128)S(1)}, f32[64,384]{1,0:T(8,128)}, u32[]{:S(2)}) copy-start(f32[64,384]{1,0:T(8,128)} %forcing_ref.1) | copy-start | bytes 294916

commit v3 on v2

--- a/solution.py
+++ b/solution.py
@@ -132,9 +132,9 @@
 
 def ghost_kernel(
     lons, lats, levels,
-    tr_ref, u_ref, v_ref, depth_ref, ocean_ref, coupling_ref,
+    tr_ref, u_ref, v_ref, depth_hbm, ocean_ref, coupling_hbm,
     g_out, rs_out, rn_out, lev_ref, cw_ref,
-    t_w, t_e, t_s, t_n, u_w, u_e, v_s, v_n,
+    depth_ref, coupling_ref, t_w, t_e, t_s, t_n, u_w, u_e, v_s, v_n,
     p_w, p_e, r_s, r_n, turned, corner_in, g_in, rs_in, rn_in,
     local_sem, send_sem, recv_sem, corner_send, corner_recv,
 ):
@@ -149,6 +149,8 @@
         pltpu.make_async_copy(src, dst, local_sem.at[i])
         for i, (src, dst) in enumerate(
             (
+                (depth_hbm, depth_ref),
+                (coupling_hbm, coupling_ref),
                 (tr_ref.at[:, :, 0:8, :], t_s),
                 (tr_ref.at[:, :, rows - 8 : rows, :], t_n),
                 (v_ref.at[:, 0:16, :], v_s),
@@ -187,6 +189,8 @@
     def _():
         rs_in[...] = jnp.zeros_like(rs_in)
 
+    for copy in locals_[0:2]:
+        copy.wait()
     row = lax.broadcasted_iota(jnp.int32, (rows, cols), 0)
     col = lane_index((rows, cols))
     tall, broad = rows // ocean_ref.shape[0], cols // ocean_ref.shape[1]
@@ -197,7 +201,7 @@
             cells = jnp.where(inside, ocean_ref[i, j], cells)
     lev_ref[...] = jnp.where(cells > 0, depth_ref[...], 0).astype(F32)
     cw_ref[...] = 6.0 + coupling_ref[...]
-    for copy in locals_[0:4]:
+    for copy in locals_[2:6]:
         copy.wait()
     tail = 8 * (lay.depth // 8)
     r_s[tail:, :] = jnp.zeros_like(r_s[tail:, :])
@@ -255,7 +259,7 @@
     pl.when(jnp.logical_not(top))(north_near.start)
     pl.when(jnp.logical_not(bottom))(south.start)
 
-    for copy in locals_[4:]:
+    for copy in locals_[6:]:
         copy.wait()
     lane = lane_index((rows, TILE))
     back = TILE - 1 - lane
@@ -324,10 +328,10 @@
 
 def column_kernel(
     levels,
-    tr_ref, u_ref, v_ref, kd_ref, lev_ref, forcing_ref, g_ref, rs_ref, rn_ref,
+    tr_ref, u_ref, v_ref, kd_ref, forcing_hbm, lev_ref, g_ref, rs_ref, rn_ref,
     out_ref, src_ref,
-    tr, u, v, kd, vx, ux, lv, mk, q, lap, sm, ratio, red, coup,
-    in_sem, out_sem,
+    forcing_ref, tr, u, v, kd, vx, ux, lv, mk, q, lap, sm, ratio, red, coup,
+    in_sem, out_sem, forcing_sem,
 ):
     lay = Layout(levels)
     rows, cols = lev_ref.shape
@@ -349,6 +353,8 @@
     for k in range(levels):
         for copy in inputs(k):
             copy.start()
+    forcing_copy = pltpu.make_async_copy(forcing_hbm, forcing_ref, forcing_sem)
+    forcing_copy.start()
     for k in range(levels):
         for a in range(2):
             s = 2 * (a * levels + k)
@@ -413,6 +419,7 @@
             wet = [mk[t, mid] for t in every]
             e, w = right(wet), left(wet)
             total = [e[t] + w[t] + mk[t, low] + mk[t, high] for t in every]
+            rate = [0.01 * x for x in wet]
             for t in every:
                 sm[t, c : c + 8] = total[t]
             for a in range(2):
@@ -420,7 +427,7 @@
                 e, w = right(centre), left(centre)
                 for t in every:
                     around = e[t] + w[t] + q[a, t, low] + q[a, t, high]
-                    lap[a, t, c : c + 8] = wet[t] * (around - centre[t] * total[t])
+                    lap[a, t, c : c + 8] = rate[t] * (around - centre[t] * total[t])
         for c in range(0, rows, 8):
             base = c + PAD
             mid, low, high = slice(base, base + 8), slice(base - 1, base + 7), slice(base + 1, base + 9)
@@ -430,36 +437,43 @@
             wet = [mk[t, mid] for t in every]
             speed = [ux[t, here] for t in every]
             wet_e, speed_e = right(wet), right(speed)
-            face = [0.25 * (speed[t] + speed_e[t]) * (wet[t] * wet_e[t]) for t in every]
+            face = [0.0625 * (speed[t] + speed_e[t]) * (wet[t] * wet_e[t]) for t in every]
             face_w = left(face)
-            wide = [[q[a, t, mid] for t in every] for a in range(2)]
-            wide_e, wide_w = [right(x) for x in wide], [left(x) for x in wide]
-            bent = [[lap[a, t, c + 1 : c + 9] for t in every] for a in range(2)]
-            bent_e, bent_w = [right(x) for x in bent], [left(x) for x in bent]
+            shared = []
             for t in range(tiles):
                 part = slice(t * TILE, (t + 1) * TILE)
                 v_mid = vx[k, t, mid]
-                v_north = 0.25 * (v_mid + vx[k, t, high]) * (wet[t] * mk[t, high])
-                v_south = 0.25 * (v_mid + vx[k, t, low]) * (wet[t] * mk[t, low])
-                spread = face[t] - face_w[t] + v_north - v_south
-                total = sm[t, c + 1 : c + 9]
+                scaled = 0.0625 * wet[t]
+                v_north = (v_mid + vx[k, t, high]) * (scaled * mk[t, high])
+                v_south = (v_mid + vx[k, t, low]) * (scaled * mk[t, low])
+                keep = 1.0 - (face[t] - face_w[t] + v_north - v_south)
                 above = coup[here, part]
                 below = jnp.where(lv[t, mid] > level + 1.0, mixing[c % 16 : c % 16 + 8, part], 0.0)
                 inverse = 1.0 / (1.0 + above + below + above * ratio[k, here, part])
                 ratio[k + 1, here, part] = -below * inverse
                 coup[here, part] = below
-                for a in range(2):
-                    centre = wide[a][t]
-                    divergence = (
-                        centre * spread
-                        + face[t] * wide_e[a][t]
-                        - face_w[t] * wide_w[a][t]
-                        + v_north * q[a, t, high]
-                        - v_south * q[a, t, low]
+                shared.append((v_north, v_south, keep, above, inverse))
+            for a in range(2):
+                wide = [q[a, t, mid] for t in every]
+                wide_e, wide_w = right(wide), left(wide)
+                partial = []
+                for t in range(tiles):
+                    v_north, v_south, keep, above, inverse = shared[t]
+                    part = slice(t * TILE, (t + 1) * TILE)
+                    partial.append(
+                        wide[t] * keep
+                        - face[t] * wide_e[t]
+                        + face_w[t] * wide_w[t]
+                        - v_north * q[a, t, high]
+                        + v_south * q[a, t, low]
                     )
-                    around = bent_e[a][t] + bent_w[a][t] + lap[a, t, c + 2 : c + 10] + lap[a, t, c : c + 8]
-                    lap_two = wet[t] * (around - bent[a][t] * total)
-                    value = centre - 0.25 * divergence - 0.01 * lap_two
+                bent = [lap[a, t, c + 1 : c + 9] for t in every]
+                bent_e, bent_w = right(bent), left(bent)
+                for t in range(tiles):
+                    v_north, v_south, keep, above, inverse = shared[t]
+                    part = slice(t * TILE, (t + 1) * TILE)
+                    around = bent_e[t] + bent_w[t] + lap[a, t, c + 2 : c + 10] + lap[a, t, c : c + 8]
+                    value = partial[t] - wet[t] * (around - bent[t] * sm[t, c + 1 : c + 9])
                     red[a, k + 1, here, part] = (value + above * red[a, k, here, part]) * inverse
         return carry
 
@@ -481,6 +495,7 @@
         return carry
 
     lax.fori_loop(0, levels - 1, up, 0)
+    forcing_copy.wait()
     src_ref[...] = jnp.where(
         lev_ref[...] > 0.0, forcing_ref[...] + coup[...] * (1.0 / levels), 0.0
     )
@@ -680,9 +695,11 @@
     ghosts, south, north, depth, weight = pl.pallas_call(
         functools.partial(ghost_kernel, lons, lats, levels),
         out_shape=(jax.ShapeDtypeStruct((2, high, TILE), F32), strip, strip, plane, plane),
-        in_specs=[HBM, HBM, HBM, VMEM, pl.BlockSpec(memory_space=pltpu.SMEM), VMEM],
+        in_specs=[HBM, HBM, HBM, HBM, pl.BlockSpec(memory_space=pltpu.SMEM), HBM],
         out_specs=(VMEM,) * 5,
         scratch_shapes=[
+            pltpu.VMEM((rows, cols), jnp.int32),
+            pltpu.VMEM((rows, cols), F32),
             pltpu.VMEM((2, levels, rows, TILE), F32),
             pltpu.VMEM((2, levels, rows, TILE), F32),
             pltpu.VMEM((2, levels, 8, cols), F32),
@@ -700,10 +717,10 @@
             pltpu.VMEM((2, rows, TILE), F32),
             pltpu.VMEM((lay.rows, cols), F32),
             pltpu.VMEM((lay.rows, cols), F32),
-            dma((8,)), dma((4,)), dma((4,)), dma((4,)), dma((4,)),
+            dma((10,)), dma((4,)), dma((4,)), dma((4,)), dma((4,)),
         ],
         compiler_params=pltpu.CompilerParams(
-            collective_id=0, has_side_effects=True, vmem_limit_bytes=32 << 20
+            collective_id=0, has_side_effects=True, vmem_limit_bytes=61 << 20
         ),
         name="ghosts",
     )(tracers, east_velocity, north_velocity, depth_levels, ocean_blocks, surface_coupling)
@@ -713,9 +730,10 @@
             jax.ShapeDtypeStruct(tracers.shape, F32),
             jax.ShapeDtypeStruct((rows, cols), F32),
         ),
-        in_specs=[HBM] * 4 + [VMEM] * 5,
+        in_specs=[HBM] * 5 + [VMEM] * 4,
         out_specs=(HBM, VMEM),
         scratch_shapes=[
+            pltpu.VMEM((rows, cols), F32),
             pltpu.VMEM((2, levels, high, wide), F32),
             pltpu.VMEM((levels, rows, cols), bf16),
             pltpu.VMEM((levels, rows, cols), bf16),
@@ -730,11 +748,11 @@
             pltpu.VMEM((levels + 1, rows, cols), F32),
             pltpu.VMEM((2, levels + 1, rows, cols), F32),
             pltpu.VMEM((rows, cols), F32),
-            dma((4, levels)), dma((levels,)),
+            dma((4, levels)), dma((levels,)), dma,
         ],
-        compiler_params=pltpu.CompilerParams(vmem_limit_bytes=48 << 20),
+        compiler_params=pltpu.CompilerParams(vmem_limit_bytes=61 << 20),
         name="columns",
-    )(tracers, east_velocity, north_velocity, vertical_diffusivity, depth, forcing, ghosts, south, north)
+    )(tracers, east_velocity, north_velocity, vertical_diffusivity, forcing, depth, ghosts, south, north)
     surface = pl.pallas_call(
         functools.partial(solve_kernel, lons, lats, levels),
         out_shape=jax.ShapeDtypeStruct((rows, cols), F32),

time: 69.7 us -> 62.9 us (0.902)
  local copies, waits for them, and re-layouts: 7.63 us -> 1.55 us
    unnamed x21 -> x13, local copies, waits for them, and re-layouts: 7.63 us -> 1.55 us
    pallas_call x1, Pallas kernels: 32.1 us -> 30.8 us  [shards(): pl.pallas_call(functools.partial(column_kernel, levels), out_shape=(jax.S...]
where the time goes in v3:
time: 62.9 us; the launch traced here: 62.7 us
  Pallas kernels  60.4 us (96%)
  local copies, waits for them, and re-layouts  1.55 us (2%)
  between operations  0.74 us (1%)
    pallas_call x1, Pallas kernels, shards(): pl.pallas_call(functools.partial(column_kernel, levels), out_shape=(jax.S...  30.8 us
    pallas_call x1, Pallas kernels, shards(): pl.pallas_call(functools.partial(solve_kernel, lons, lats, levels), out_s...  15.6 us
    pallas_call x1, Pallas kernels, shards(): pl.pallas_call(functools.partial(ghost_kernel, lons, lats, levels), out_s...  14 us
    unnamed x13, local copies, waits for them, and re-layouts  1.55 us

profile of v3, /device:TPU:0, one launch (start us, length us, event | category | flops | bytes accessed | tf_op | source)
XLA Modules:
  0.0 62.7 jit_solution(17977419917482908463)
XLA Ops:
  0.6 14.0 %ghosts.1 = (f32[2,80,128]{2,1,0:T(8,128)}, f32[112,384]{1,0:T(8,128)}, f32[112,384]{1,0:T(8,128)}, f32[64,384]{1,0:T(8,128)}, f32[64,384]{1,0:T(8,128)}) custom-call(f32[2,20,64,384]{3,2,1,0:T(8,128)} %tr_ref.3, bf16[20,64,384]{2,1,0:T(8,128)(2,1)} %u_ref.3, bf16[20,64,384]{2,1,0:T(8,128)(2,1)} %v_ref.3, s32[64,384]{1,0:T(8,128)} %depth_hbm.1, ...), custom_call_target="tpu_custom_call" | custom-call | tf_op jit(solution)/shard_map/ghosts/pallas_call | solution.py:695
  14.6 0.0 copy-start
  14.6 0.0 copy-start.1
  14.6 0.0 copy-start.2
  14.7 0.0 copy-start.3
  14.7 0.0 copy-start.4
  14.7 30.8 %columns.1 = (f32[2,20,64,384]{3,2,1,0:T(8,128)}, f32[64,384]{1,0:T(8,128)}) custom-call(f32[2,20,64,384]{3,2,1,0:T(8,128)} %tr_ref.3, bf16[20,64,384]{2,1,0:T(8,128)(2,1)} %u_ref.3, bf16[20,64,384]{2,1,0:T(8,128)(2,1)} %v_ref.3, bf16[20,64,384]{2,1,0:T(8,128)(2,1)} %kd_ref.1, f32[64,384]{1,0:T(8,128)} %forcing_hbm.1, f32[64,384]{1,0:T(8,128)} %get-tuple-element.9.lev_ref, ...), custom_call_target="tpu_custom_call" | custom-call | tf_op jit(solution)/shard_map/columns/pallas_call | solution.py:727
  45.5 0.0 copy-done
  45.5 0.0 copy-done.1
  45.5 0.0 copy-done.2
  45.5 0.0 copy-done.3
  45.5 0.0 copy-done.4
  45.5 0.0 copy-start.5
  45.5 0.9 %copy-done.5 = f32[64,384]{1,0:T(8,128)S(1)} copy-done((f32[64,384]{1,0:T(8,128)S(1)}, f32[64,384]{1,0:T(8,128)}, u32[]{:S(2)}) %copy-start.5) | copy-done | bytes 98328
  46.4 15.6 %surface.1 = f32[64,384]{1,0:T(8,128)S(1)} custom-call(f32[64,384]{1,0:T(8,128)S(1)} %copy-done.5, f32[64,384]{1,0:T(8,128)S(1)} %copy-done.2, f32[64,384]{1,0:T(8,128)S(1)} %copy-done.4, f32[2,80,128]{2,1,0:T(8,128)S(1)} %copy-done.3, f32[112,384]{1,0:T(8,128)S(1)} %copy-done, f32[112,384]{1,0:T(8,128)S(1)} %copy-done.1), custom_call_target="tpu_custom_call" | custom-call | tf_op jit(solution)/shard_map/surface/pallas_call | solution.py:756
  62.1 0.6 %copy.11 = f32[64,384]{1,0:T(8,128)} copy(f32[64,384]{1,0:T(8,128)S(1)} %surface.1) | data formatting | bytes 196608
Async XLA Ops:
  14.6 30.9 %copy-start = (f32[112,384]{1,0:T(8,128)S(1)}, f32[112,384]{1,0:T(8,128)}, u32[]{:S(2)}) copy-start(f32[112,384]{1,0:T(8,128)} %get-tuple-element.11.rs_ref) | copy-start | bytes 516100
  14.6 30.9 %copy-start.1 = (f32[112,384]{1,0:T(8,128)S(1)}, f32[112,384]{1,0:T(8,128)}, u32[]{:S(2)}) copy-start(f32[112,384]{1,0:T(8,128)} %get-tuple-element.12.rn_ref) | copy-start | bytes 516100
  14.6 30.9 %copy-start.2 = (f32[64,384]{1,0:T(8,128)S(1)}, f32[64,384]{1,0:T(8,128)}, u32[]{:S(2)}) copy-start(f32[64,384]{1,0:T(8,128)} %get-tuple-element.9.lev_ref) | copy-start | bytes 294916
  14.7 30.9 %copy-start.3 = (f32[2,80,128]{2,1,0:T(8,128)S(1)}, f32[2,80,128]{2,1,0:T(8,128)}, u32[]{:S(2)}) copy-start(f32[2,80,128]{2,1,0:T(8,128)} %get-tuple-element.10.g_ref) | copy-start | bytes 245764
  14.7 30.9 %copy-start.4 = (f32[64,384]{1,0:T(8,128)S(1)}, f32[64,384]{1,0:T(8,128)}, u32[]{:S(2)}) copy-start(f32[64,384]{1,0:T(8,128)} %get-tuple-element.15.cw_ref) | copy-start | bytes 294916
  45.5 0.9 %copy-start.5 = (f32[64,384]{1,0:T(8,128)S(1)}, f32[64,384]{1,0:T(8,128)}, u32[]{:S(2)}) copy-start(f32[64,384]{1,0:T(8,128)} %get-tuple-element.14.src_ref) | copy-start | bytes 294916

commit v4 on v3

--- a/solution.py
+++ b/solution.py
@@ -477,7 +477,9 @@
                     red[a, k + 1, here, part] = (value + above * red[a, k, here, part]) * inverse
         return carry
 
-    lax.fori_loop(0, levels, down, 0)
+    lax.fori_loop(0, levels // 2, lambda i, c: down(2 * i + 1, down(2 * i, c)), 0)
+    if levels % 2:
+        down(jnp.int32(levels - 1), 0)
     outputs(levels - 1).start()
     coup[...] = red[0, levels] - red[1, levels]
 
@@ -505,13 +507,15 @@
 
 def solve_kernel(
     lons, lats, levels,
-    src_ref, lev_ref, cw_ref, g_ref, rs_ref, rn_ref,
+    src_hbm, lev_ref, cw_ref, g_ref, rs_ref, rn_ref,
     out_ref,
-    lv, cw, bx, side_in, row_n, row_in, corner_in, part, lon_in, joint, lat_in,
+    src_ref, src_sem, lv, cw, bx, side_in, row_n, row_in, corner_in, part, lon_in, joint, lat_in,
     send_sem, recv_sem, corner_send, corner_recv, lon_send, lon_recv, lat_send, lat_recv,
 ):
     lay = Layout(levels)
     rows, cols = src_ref.shape
+    src_copy = pltpu.make_async_copy(src_hbm, src_ref, src_sem)
+    src_copy.start()
     lon, lat = lax.axis_index("lon"), lax.axis_index("lat")
     east, west = lax.rem(lon + 1, lons), lax.rem(lon + lons - 1, lons)
     mirror = lons - 1 - lon
@@ -537,6 +541,8 @@
     def _():
         greet(barrier, east, lat - 1)
         greet(barrier, west, lat - 1)
+
+    src_copy.wait()
 
     @pl.when(jnp.logical_not(top))
     def _():
@@ -756,9 +762,11 @@
     surface = pl.pallas_call(
         functools.partial(solve_kernel, lons, lats, levels),
         out_shape=jax.ShapeDtypeStruct((rows, cols), F32),
-        in_specs=[VMEM] * 6,
+        in_specs=[HBM] + [VMEM] * 5,
         out_specs=VMEM,
         scratch_shapes=[
+            pltpu.VMEM((rows, cols), F32),
+            dma,
             pltpu.VMEM((high, wide), F32),
             pltpu.VMEM((high, wide), F32),
             pltpu.VMEM((high, wide), F32),

time: 62.9 us -> 63.1 us (level)
  no operation moved by 1% of the time
where the time goes in v4:
time: 63.1 us; the launch traced here: 63 us
  Pallas kernels  60.7 us (96%)
  local copies, waits for them, and re-layouts  1.55 us (2%)
  between operations  0.74 us (1%)
    pallas_call x1, Pallas kernels, shards(): pl.pallas_call(functools.partial(column_kernel, levels), out_shape=(jax.S...  30.8 us
    pallas_call x1, Pallas kernels, shards(): pl.pallas_call(functools.partial(solve_kernel, lons, lats, levels), out_s...  15.8 us
    pallas_call x1, Pallas kernels, shards(): pl.pallas_call(functools.partial(ghost_kernel, lons, lats, levels), out_s...  14 us
    unnamed x13, local copies, waits for them, and re-layouts  1.55 us

profile of v4, /device:TPU:0, one launch (start us, length us, event | category | flops | bytes accessed | tf_op | source)
XLA Modules:
  0.0 63.0 jit_solution(467653101769624504)
XLA Ops:
  0.6 14.0 %ghosts.1 = (f32[2,80,128]{2,1,0:T(8,128)}, f32[112,384]{1,0:T(8,128)}, f32[112,384]{1,0:T(8,128)}, f32[64,384]{1,0:T(8,128)}, f32[64,384]{1,0:T(8,128)}) custom-call(f32[2,20,64,384]{3,2,1,0:T(8,128)} %tr_ref.3, bf16[20,64,384]{2,1,0:T(8,128)(2,1)} %u_ref.3, bf16[20,64,384]{2,1,0:T(8,128)(2,1)} %v_ref.3, s32[64,384]{1,0:T(8,128)} %depth_hbm.1, ...), custom_call_target="tpu_custom_call" | custom-call | tf_op jit(solution)/shard_map/ghosts/pallas_call | solution.py:701
  14.6 0.0 copy-start
  14.6 0.0 copy-start.1
  14.6 0.0 copy-start.2
  14.7 0.0 copy-start.3
  14.7 0.0 copy-start.4
  14.7 30.8 %columns.1 = (f32[2,20,64,384]{3,2,1,0:T(8,128)}, f32[64,384]{1,0:T(8,128)}) custom-call(f32[2,20,64,384]{3,2,1,0:T(8,128)} %tr_ref.3, bf16[20,64,384]{2,1,0:T(8,128)(2,1)} %u_ref.3, bf16[20,64,384]{2,1,0:T(8,128)(2,1)} %v_ref.3, bf16[20,64,384]{2,1,0:T(8,128)(2,1)} %kd_ref.1, f32[64,384]{1,0:T(8,128)} %forcing_hbm.1, f32[64,384]{1,0:T(8,128)} %get-tuple-element.9.lev_ref, ...), custom_call_target="tpu_custom_call" | custom-call | tf_op jit(solution)/shard_map/columns/pallas_call | solution.py:733
  45.5 0.0 copy-done
  45.5 0.0 copy-done.1
  45.5 0.0 copy-done.2
  45.5 0.0 copy-done.3
  45.6 0.0 copy-done.4
  45.6 0.0 copy-start.5
  45.6 0.9 %copy-done.5 = f32[64,384]{1,0:T(8,128)S(1)} copy-done((f32[64,384]{1,0:T(8,128)S(1)}, f32[64,384]{1,0:T(8,128)}, u32[]{:S(2)}) %copy-start.5) | copy-done | bytes 98328
  46.5 15.8 %surface.1 = f32[64,384]{1,0:T(8,128)S(1)} custom-call(f32[64,384]{1,0:T(8,128)S(1)} %copy-done.5, f32[64,384]{1,0:T(8,128)S(1)} %copy-done.2, f32[64,384]{1,0:T(8,128)S(1)} %copy-done.4, f32[2,80,128]{2,1,0:T(8,128)S(1)} %copy-done.3, f32[112,384]{1,0:T(8,128)S(1)} %copy-done, f32[112,384]{1,0:T(8,128)S(1)} %copy-done.1), custom_call_target="tpu_custom_call" | custom-call | tf_op jit(solution)/shard_map/surface/pallas_call | solution.py:762
  62.3 0.6 %copy.11 = f32[64,384]{1,0:T(8,128)} copy(f32[64,384]{1,0:T(8,128)S(1)} %surface.1) | data formatting | bytes 196608
Async XLA Ops:
  14.6 30.9 %copy-start = (f32[112,384]{1,0:T(8,128)S(1)}, f32[112,384]{1,0:T(8,128)}, u32[]{:S(2)}) copy-start(f32[112,384]{1,0:T(8,128)} %get-tuple-element.11.rs_ref) | copy-start | bytes 516100
  14.6 30.9 %copy-start.1 = (f32[112,384]{1,0:T(8,128)S(1)}, f32[112,384]{1,0:T(8,128)}, u32[]{:S(2)}) copy-start(f32[112,384]{1,0:T(8,128)} %get-tuple-element.12.rn_ref) | copy-start | bytes 516100
  14.6 30.9 %copy-start.2 = (f32[64,384]{1,0:T(8,128)S(1)}, f32[64,384]{1,0:T(8,128)}, u32[]{:S(2)}) copy-start(f32[64,384]{1,0:T(8,128)} %get-tuple-element.9.lev_ref) | copy-start | bytes 294916
  14.7 30.9 %copy-start.3 = (f32[2,80,128]{2,1,0:T(8,128)S(1)}, f32[2,80,128]{2,1,0:T(8,128)}, u32[]{:S(2)}) copy-start(f32[2,80,128]{2,1,0:T(8,128)} %get-tuple-element.10.g_ref) | copy-start | bytes 245764
  14.7 30.9 %copy-start.4 = (f32[64,384]{1,0:T(8,128)S(1)}, f32[64,384]{1,0:T(8,128)}, u32[]{:S(2)}) copy-start(f32[64,384]{1,0:T(8,128)} %get-tuple-element.15.cw_ref) | copy-start | bytes 294916
  45.6 0.9 %copy-start.5 = (f32[64,384]{1,0:T(8,128)S(1)}, f32[64,384]{1,0:T(8,128)}, u32[]{:S(2)}) copy-start(f32[64,384]{1,0:T(8,128)} %get-tuple-element.14.src_hbm) | copy-start | bytes 294916
